TPU v7x, 32 devices: a whole 2x2x4 slice. The times are simulated.
32 devices in a mesh: groups: 1, along: 8 (over z, y), across: 4 (over x, core).
Axes of the slice: x: 2, y: 2, z: 4, core: 2. Of those that a mesh axis runs over, the one named last changes fastest.
Arguments:
- doses: float32 [8, 4, 512], P(('groups', 'along'), 'across'), may hold values from 0.1 to 10
- shot_type: int32 [8, 4, 512], P(('groups', 'along'), 'across'), may hold values from 0 to 7
- shot_count: int32 [8, 4], P(('groups', 'along'), 'across'), may hold values from 1 to 512, as said below
- dose_weights: bfloat16 [8, 2048, 512], P(None, ('groups', 'along'), 'across'), may hold values from 0.019897461 to 1
- cotangent: float32 [2048, 512], P(('groups', 'along'), 'across'), may hold values from -6 to 6
Outputs:
- exposure: float32 [2048, 512], P(('groups', 'along'), 'across')
- dose_grad: float32 [8, 4, 512], P(('groups', 'along'), 'across')
Inputs may be any that keep to these rules, and one draw needn't show every extreme that they name: Shot slots 0 to shot_count - 1 of a tile are live; some tile has all 512 live, some tile only one.
All inputs are finite; a program needn't handle non-finite values.
Results may differ from a plain program's by a relative error of at most 0.0003.
Values sent between devices are 32-bit elements; how exact they have to be, the bound alone decides.
A program may use at most 64 MiB of HBM per device.

v0:
```python
import math

import jax
import jax.numpy as jnp
from jax import lax
from jax.sharding import PartitionSpec as P

H = 16


sigma_fine = 3.75
sigma_back = 156.25
back_ratio = 0.7
exact = lax.Precision.HIGHEST


def extended(cells, sides, width):
    for axis, dim in sides:
        count = lax.axis_size(axis)
        ends = count - 1
        head = lax.slice_in_dim(cells, 0, width, axis=dim)
        tail = lax.slice_in_dim(cells, cells.shape[dim] - width, cells.shape[dim], axis=dim)
        cells = jnp.concatenate(
            [
                lax.ppermute(tail, axis, [(i, (i + 1) % count) for i in range(ends)]),
                cells,
                lax.ppermute(head, axis, [((i + 1) % count, i) for i in range(ends)]),
            ],
            axis=dim,
        )
    return cells


def fine_weights(offsets):
    reach = jnp.arange(-H, H + 1).astype(jnp.float32)
    norm_total = jnp.sum(jnp.exp(-reach * reach / (2.0 * sigma_fine * sigma_fine)))
    inside = jnp.abs(offsets) <= H
    return jnp.where(
        inside, jnp.exp(-offsets * offsets / (2.0 * sigma_fine * sigma_fine)) / norm_total, 0.0
    )


def fine_band(length):
    row_index = lax.broadcasted_iota(jnp.int32, (length, length + 2 * H), 0)
    col_index = lax.broadcasted_iota(jnp.int32, (length, length + 2 * H), 1)
    return fine_weights((col_index - row_index - H).astype(jnp.float32))


def blur_fine(field):
    row_count, col_count = field.shape
    band_rows = fine_band(row_count)
    band_cols = fine_band(col_count)
    padded = extended(field, (("along", 0), ("across", 1)), H)
    middle = jnp.dot(band_rows, padded, precision=exact)
    return jnp.dot(middle, band_cols.T, precision=exact)


def back_weights(distance):
    return jnp.exp(-distance * distance / (2.0 * sigma_back * sigma_back)) / (
        math.sqrt(2.0 * math.pi) * sigma_back
    )


def blur_back(field):
    row_count, col_count = field.shape
    coarse = field.reshape(row_count // 8, 8, col_count // 8, 8).mean(axis=(1, 3))
    coarse_rows, coarse_cols = coarse.shape
    mine_rows = (
        lax.axis_index("along") * coarse_rows + lax.broadcasted_iota(jnp.int32, (coarse_rows,), 0)
    ).astype(jnp.float32)
    mine_cols = (
        lax.axis_index("across") * coarse_cols + lax.broadcasted_iota(jnp.int32, (coarse_cols,), 0)
    ).astype(jnp.float32)
    piece = lax.all_gather(coarse, "along", axis=0, tiled=True)
    theirs = lax.broadcasted_iota(jnp.int32, (piece.shape[0],), 0).astype(jnp.float32)
    kernel = back_weights(mine_rows[:, None] - theirs[None, :])
    along_blur = jnp.dot(kernel, piece, precision=exact)
    piece = lax.all_gather(along_blur, "across", axis=1, tiled=True)
    theirs = lax.broadcasted_iota(jnp.int32, (piece.shape[1],), 0).astype(jnp.float32)
    kernel = back_weights(theirs[:, None] - mine_cols[None, :])
    both_blur = jnp.dot(piece, kernel, precision=exact)
    spread = jnp.broadcast_to(both_blur[:, None, :, None], (coarse_rows, 8, coarse_cols, 8))
    return spread.reshape(row_count, col_count)


def operator_apply(field):
    return blur_fine(field) + back_ratio * blur_back(field)


def dose_map(coef, dose_weights):
    total = coef[0] * dose_weights[0].astype(jnp.float32)
    for kind in range(1, dose_weights.shape[0]):
        total = total + coef[kind] * dose_weights[kind].astype(jnp.float32)
    return total


def weighted(dose_weights, field):
    return jnp.stack(
        [
            jnp.sum(dose_weights[kind].astype(jnp.float32) * field)
            for kind in range(dose_weights.shape[0])
        ]
    )


def shards(doses, shot_type, shot_count, dose_weights, cotangent):
    kinds = dose_weights.shape[0]
    shots = doses.shape[-1]
    live = (lax.broadcasted_iota(jnp.int32, (shots,), 0) < shot_count.reshape(())).astype(
        jnp.float32
    )
    onehot = (
        shot_type.reshape(shots)[:, None] == lax.broadcasted_iota(jnp.int32, (shots, kinds), 1)
    ).astype(jnp.float32)
    share = kinds / shots
    coef = share * jnp.sum(onehot * (live * doses.reshape(shots))[:, None], axis=0)
    totals = jnp.stack([jnp.sum(dose_weights[kind].astype(jnp.float32)) for kind in range(kinds)])
    coefs = [coef]
    ratios = []
    for section in range(2):
        field = operator_apply(dose_map(coefs[-1], dose_weights))
        ratio = weighted(dose_weights, field) / totals
        ratios.append(ratio)
        coefs.append(coefs[-1] / ratio)
    final_field = operator_apply(dose_map(coefs[2], dose_weights))
    grad_coef = weighted(dose_weights, operator_apply(cotangent))
    for section in (1, 0):
        grad_ratio = -grad_coef * coefs[section + 1] / ratios[section]
        grad_coef = grad_coef / ratios[section]
        grad_field = dose_map(grad_ratio / totals, dose_weights)
        grad_coef = grad_coef + weighted(dose_weights, operator_apply(grad_field))
    grad_doses = live * share * jnp.dot(onehot, grad_coef, precision=exact)
    return (final_field, grad_doses.reshape(doses.shape))


def solution(mesh):
    in_specs = (
        P(("groups", "along"), "across", None),
        P(("groups", "along"), "across", None),
        P(("groups", "along"), "across"),
        P(None, ("groups", "along"), "across"),
        P(("groups", "along"), "across"),
    )
    out_specs = (P(("groups", "along"), "across"), P(("groups", "along"), "across", None))
    return jax.shard_map(shards, mesh=mesh, in_specs=in_specs, out_specs=out_specs, check_vma=False)
```

profile of v0, /device:TPU:0, one launch (start us, length us, event | category | flops | bytes accessed | tf_op | source)
XLA Modules:
  0.0 427.2 jit_solution(9142940627251713966)
XLA Ops:
  3.5 6.2 %fusion.156 = f32[256,128]{1,0:T(8,128)S(1)} fusion(f32[]{:T(128)} %bitcast.25, f32[]{:T(128)} %bitcast.23, f32[]{:T(128)} %bitcast.21, f32[]{:T(128)} %bitcast.19, f32[]{:T(128)} %bitcast.17, f32[]{:T(128)} %bitcast.15, f32[]{:T(128)} %bitcast.13, f32[]{:T(128)} %bitcast.12, bf16[8,256,128]{2,1,0:T(8,128)(2,1)} %param.8), kind=kLoop, calls=%fused_computation.226 | loop fusion | flops 753664 | bytes 655392 | tf_op jit(solution)/shard_map/add | solution.py:93
  9.7 1.3 collective-permute-start.1
  11.0 5.5 %collective-permute-start = (f32[16,128]{1,0:T(8,128)S(1)}, f32[16,128]{1,0:T(8,128)S(1)}, u32[]{:S(2)}, u32[]{:S(2)}) collective-permute-start(f32[16,128]{1,0:T(8,128)S(1)} %get-tuple-element.80), channel_id=1, source_target_pairs={{0,4},{4,8},{8,12},{12,16},{16,20},{20,24},{24,28},{1,5},{5,9},{9,... | collective-permute-start | bytes 24584 | tf_op jit(solution)/shard_map/ppermute | solution.py:25
  17.2 4.8 %collective-permute-start.12 = (f32[16,128]{1,0:T(8,128)S(1)}, f32[16,128]{1,0:T(8,128)S(1)}, u32[]{:S(2)}, u32[]{:S(2)}) collective-permute-start(f32[16,128]{1,0:T(8,128)S(1)} %get-tuple-element.83), channel_id=1, source_target_pairs={{0,4},{4,8},{8,12},{12,16},{16,20},{20,24},{24,28},{1,5},{5,9},{9,... | collective-permute-start | bytes 24584 | tf_op jit(solution)/shard_map/ppermute | solution.py:25
  22.0 1.3 collective-permute-start.13
  23.3 6.2 %fusion.196 = f32[1,256,128]{2,1,0:T(8,128)S(1)} fusion(f32[]{:T(128)} %bitcast.25, f32[]{:T(128)} %bitcast.23, f32[]{:T(128)} %bitcast.21, f32[]{:T(128)} %bitcast.19, f32[]{:T(128)} %bitcast.17, f32[]{:T(128)} %bitcast.15, f32[]{:T(128)} %bitcast.13, f32[]{:T(128)} %bitcast.12, bf16[8,256,128]{2,1,0:T(8,128)(2,1)} %param.8), kind=kLoop, calls=%fused_computation.266 | loop fusion | flops 753664 | bytes 655392 | tf_op jit(solution)/shard_map/add | solution.py:93
  29.5 2.1 reshape.221
  31.7 2.5 reshape.243
  34.2 1.8 reduce_sum.558
  36.1 32.1 %all-gather = f32[8,32,16]{1,2,0:T(8,128)S(1)} all-gather(f32[1,32,16]{1,2,0:T(8,128)S(1)} %copy.55), channel_id=1, replica_groups=mesh['groups'=1,'along'=8,'across'=4] {'along'}, dimensions={0}, use_global_device_ids=true | all-gather | bytes 18432 | tf_op jit(solution)/shard_map/all_gather | solution.py:74
  68.5 5.2 %all_gather.37 = f32[32,64]{0,1:T(8,128)S(1)} all-gather(f32[32,16]{0,1:T(8,128)S(1)} %fusion.288), channel_id=1, replica_groups=mesh['groups'=1,'along'=8,'across'=4] {'across'}, dimensions={1}, use_global_device_ids=true | all-gather | bytes 10240 | tf_op jit(solution)/shard_map/all_gather | solution.py:78
  74.0 30.5 %all-gather.3 = f32[8,32,16]{1,2,0:T(8,128)S(1)} all-gather(f32[1,32,16]{1,2,0:T(8,128)S(1)} %copy.64), channel_id=1, replica_groups=mesh['groups'=1,'along'=8,'across'=4] {'along'}, dimensions={0}, use_global_device_ids=true | all-gather | bytes 18432 | tf_op jit(solution)/shard_map/all_gather | solution.py:74
  104.8 5.2 %all_gather.43 = f32[32,64]{0,1:T(8,128)S(1)} all-gather(f32[32,16]{0,1:T(8,128)S(1)} %fusion.282), channel_id=1, replica_groups=mesh['groups'=1,'along'=8,'across'=4] {'across'}, dimensions={1}, use_global_device_ids=true | all-gather | bytes 10240 | tf_op jit(solution)/shard_map/all_gather | solution.py:78
  112.9 1.6 mul.1090
  114.6 5.0 %stack.170 = f32[8]{0:T(128)S(1)} concatenate(f32[1]{0:T(128)} %bitcast.3, f32[1]{0:T(128)} %bitcast.4, f32[1]{0:T(128)} %bitcast.5, f32[1]{0:T(128)} %bitcast.6, f32[1]{0:T(128)} %bitcast.7, f32[1]{0:T(128)} %bitcast.8, f32[1]{0:T(128)} %bitcast.9, f32[1]{0:T(128)} %bitcast.10), dimensions={0} | concatenate | bytes 64 | tf_op jit(solution)/shard_map/stack | solution.py:117
  120.3 1.3 collective-permute-start.3
  121.6 3.0 collective-permute-start.2
  124.8 1.3 collective-permute-start.15
  126.1 4.8 %collective-permute-start.14 = (f32[288,16]{1,0:T(8,128)S(1)}, f32[288,16]{1,0:T(8,128)}, u32[]{:S(2)}, u32[]{:S(2)}) collective-permute-start(f32[288,16]{1,0:T(8,128)S(1)} %get-tuple-element.70), channel_id=1, source_target_pairs={{0,1},{1,2},{2,3},{4,5},{5,6},{6,7},{8,9},{9,10},{10,11},{12,13},{... | collective-permute-start | bytes 55304 | tf_op jit(solution)/shard_map/ppermute | solution.py:25
  130.9 1.6 fusion.84
  132.5 2.1 fusion.255
  134.6 5.1 %stack.179 = f32[8]{0:T(128)S(1)} concatenate(f32[1]{0:T(128)} %bitcast.28, f32[1]{0:T(128)} %bitcast.29, f32[1]{0:T(128)} %bitcast.30, f32[1]{0:T(128)} %bitcast.31, f32[1]{0:T(128)} %bitcast.32, f32[1]{0:T(128)} %bitcast.33, f32[1]{0:T(128)} %bitcast.34, f32[1]{0:T(128)} %bitcast.35), dimensions={0} | concatenate | bytes 64 | tf_op jit(solution)/shard_map/stack | solution.py:98
  140.3 5.1 %fusion.203 = f32[1,256,128]{2,1,0:T(8,128)S(1)} fusion(f32[]{:T(128)} %bitcast.43, f32[]{:T(128)} %bitcast.42, f32[]{:T(128)} %bitcast.41, f32[]{:T(128)} %bitcast.40, f32[]{:T(128)} %bitcast.39, f32[]{:T(128)} %bitcast.38, f32[]{:T(128)} %bitcast.37, f32[]{:T(128)} %bitcast.36, bf16[8,256,128]{2,1,0:T(8,128)(2,1)S(1)} %copy-done), kind=kLoop, calls=%fused_computation.273 | loop fusion | flops 753664 | bytes 655392 | tf_op jit(solution)/shard_map/add | solution.py:93
  145.4 5.1 %fusion.164 = f32[256,128]{1,0:T(8,128)S(1)} fusion(f32[]{:T(128)} %bitcast.43, f32[]{:T(128)} %bitcast.42, f32[]{:T(128)} %bitcast.41, f32[]{:T(128)} %bitcast.40, f32[]{:T(128)} %bitcast.39, f32[]{:T(128)} %bitcast.38, f32[]{:T(128)} %bitcast.37, f32[]{:T(128)} %bitcast.36, bf16[8,256,128]{2,1,0:T(8,128)(2,1)S(1)} %copy-done), kind=kLoop, calls=%fused_computation.234 | loop fusion | flops 753664 | bytes 655392 | tf_op jit(solution)/shard_map/add | solution.py:93
  151.9 30.5 %all-gather.1 = f32[8,32,16]{1,2,0:T(8,128)S(1)} all-gather(f32[1,32,16]{1,2,0:T(8,128)S(1)} %copy.58), channel_id=1, replica_groups=mesh['groups'=1,'along'=8,'across'=4] {'along'}, dimensions={0}, use_global_device_ids=true | all-gather | bytes 18432 | tf_op jit(solution)/shard_map/all_gather | solution.py:74
  182.8 5.2 %all_gather.39 = f32[32,64]{0,1:T(8,128)S(1)} all-gather(f32[32,16]{0,1:T(8,128)S(1)} %fusion.286), channel_id=1, replica_groups=mesh['groups'=1,'along'=8,'across'=4] {'across'}, dimensions={1}, use_global_device_ids=true | all-gather | bytes 10240 | tf_op jit(solution)/shard_map/all_gather | solution.py:78
  189.2 4.5 %collective-permute-start.4 = (f32[16,128]{1,0:T(8,128)S(1)}, f32[16,128]{1,0:T(8,128)S(1)}, u32[]{:S(2)}, u32[]{:S(2)}) collective-permute-start(f32[16,128]{1,0:T(8,128)S(1)} %get-tuple-element.78), channel_id=1, source_target_pairs={{0,4},{4,8},{8,12},{12,16},{16,20},{20,24},{24,28},{1,5},{5,9},{9,... | collective-permute-start | bytes 24584 | tf_op jit(solution)/shard_map/ppermute | solution.py:25
  197.2 3.7 collective-permute-start.6
  200.9 3.2 fusion.114
  205.4 2.6 fusion.94
  208.0 1.3 convolution_add_fusion.4
  209.4 2.1 fusion.257
  211.5 5.1 %stack.188 = f32[8]{0:T(128)S(1)} concatenate(f32[1]{0:T(128)} %bitcast.45, f32[1]{0:T(128)} %bitcast.46, f32[1]{0:T(128)} %bitcast.47, f32[1]{0:T(128)} %bitcast.48, f32[1]{0:T(128)} %bitcast.49, f32[1]{0:T(128)} %bitcast.50, f32[1]{0:T(128)} %bitcast.51, f32[1]{0:T(128)} %bitcast.52), dimensions={0} | concatenate | bytes 64 | tf_op jit(solution)/shard_map/stack | solution.py:98
  216.5 5.0 %stack.197 = f32[8]{0:T(128)S(1)} concatenate(f32[1]{0:T(128)} %bitcast.63, f32[1]{0:T(128)} %bitcast.64, f32[1]{0:T(128)} %bitcast.65, f32[1]{0:T(128)} %bitcast.66, f32[1]{0:T(128)} %bitcast.67, f32[1]{0:T(128)} %bitcast.68, f32[1]{0:T(128)} %bitcast.69, f32[1]{0:T(128)} %bitcast.70), dimensions={0} | concatenate | bytes 64 | tf_op jit(solution)/shard_map/stack | solution.py:98
  222.3 5.1 %fusion.210 = f32[1,256,128]{2,1,0:T(8,128)S(1)} fusion(f32[]{:T(128)} %bitcast.60, f32[]{:T(128)} %bitcast.59, f32[]{:T(128)} %bitcast.58, f32[]{:T(128)} %bitcast.57, f32[]{:T(128)} %bitcast.56, f32[]{:T(128)} %bitcast.55, f32[]{:T(128)} %bitcast.54, f32[]{:T(128)} %bitcast.53, bf16[8,256,128]{2,1,0:T(8,128)(2,1)S(1)} %copy-done), kind=kLoop, calls=%fused_computation.280 | loop fusion | flops 753664 | bytes 655392 | tf_op jit(solution)/shard_map/add | solution.py:93
  227.4 5.1 %fusion.172 = f32[256,128]{1,0:T(8,128)S(1)} fusion(f32[]{:T(128)} %bitcast.60, f32[]{:T(128)} %bitcast.59, f32[]{:T(128)} %bitcast.58, f32[]{:T(128)} %bitcast.57, f32[]{:T(128)} %bitcast.56, f32[]{:T(128)} %bitcast.55, f32[]{:T(128)} %bitcast.54, f32[]{:T(128)} %bitcast.53, bf16[8,256,128]{2,1,0:T(8,128)(2,1)S(1)} %copy-done), kind=kLoop, calls=%fused_computation.242 | loop fusion | flops 753664 | bytes 655392 | tf_op jit(solution)/shard_map/add | solution.py:93
  232.5 5.0 %fusion.217 = f32[1,256,128]{2,1,0:T(8,128)S(1)} fusion(f32[]{:T(128)} %bitcast.78, f32[]{:T(128)} %bitcast.77, f32[]{:T(128)} %bitcast.76, f32[]{:T(128)} %bitcast.75, f32[]{:T(128)} %bitcast.74, f32[]{:T(128)} %bitcast.73, f32[]{:T(128)} %bitcast.72, f32[]{:T(128)} %bitcast.71, bf16[8,256,128]{2,1,0:T(8,128)(2,1)S(1)} %copy-done), kind=kLoop, calls=%fused_computation.287 | loop fusion | flops 753664 | bytes 655392 | tf_op jit(solution)/shard_map/add | solution.py:93
  237.6 5.0 %fusion.180 = f32[256,128]{1,0:T(8,128)S(1)} fusion(f32[]{:T(128)} %bitcast.78, f32[]{:T(128)} %bitcast.77, f32[]{:T(128)} %bitcast.76, f32[]{:T(128)} %bitcast.75, f32[]{:T(128)} %bitcast.74, f32[]{:T(128)} %bitcast.73, f32[]{:T(128)} %bitcast.72, f32[]{:T(128)} %bitcast.71, bf16[8,256,128]{2,1,0:T(8,128)(2,1)S(1)} %copy-done), kind=kLoop, calls=%fused_computation.250 | loop fusion | flops 753664 | bytes 655392 | tf_op jit(solution)/shard_map/add | solution.py:93
  244.0 30.5 %all-gather.2 = f32[8,32,16]{1,2,0:T(8,128)S(1)} all-gather(f32[1,32,16]{1,2,0:T(8,128)S(1)} %copy.61), channel_id=1, replica_groups=mesh['groups'=1,'along'=8,'across'=4] {'along'}, dimensions={0}, use_global_device_ids=true | all-gather | bytes 18432 | tf_op jit(solution)/shard_map/all_gather | solution.py:74
  274.9 5.2 %all_gather.41 = f32[32,64]{0,1:T(8,128)S(1)} all-gather(f32[32,16]{0,1:T(8,128)S(1)} %fusion.284), channel_id=1, replica_groups=mesh['groups'=1,'along'=8,'across'=4] {'across'}, dimensions={1}, use_global_device_ids=true | all-gather | bytes 10240 | tf_op jit(solution)/shard_map/all_gather | solution.py:78
  281.7 1.3 collective-permute-start.9
  283.0 4.5 %collective-permute-start.8 = (f32[16,128]{1,0:T(8,128)S(1)}, f32[16,128]{1,0:T(8,128)S(1)}, u32[]{:S(2)}, u32[]{:S(2)}) collective-permute-start(f32[16,128]{1,0:T(8,128)S(1)} %get-tuple-element.76), channel_id=1, source_target_pairs={{0,4},{4,8},{8,12},{12,16},{16,20},{20,24},{24,28},{1,5},{5,9},{9,... | collective-permute-start | bytes 24584 | tf_op jit(solution)/shard_map/ppermute | solution.py:25
  289.0 30.5 %all-gather.4 = f32[8,32,16]{1,2,0:T(8,128)S(1)} all-gather(f32[1,32,16]{1,2,0:T(8,128)S(1)} %copy.67), channel_id=1, replica_groups=mesh['groups'=1,'along'=8,'across'=4] {'along'}, dimensions={0}, use_global_device_ids=true | all-gather | bytes 18432 | tf_op jit(solution)/shard_map/all_gather | solution.py:74
  319.8 5.2 %all_gather.45 = f32[32,64]{0,1:T(8,128)S(1)} all-gather(f32[32,16]{0,1:T(8,128)S(1)} %fusion.280), channel_id=1, replica_groups=mesh['groups'=1,'along'=8,'across'=4] {'across'}, dimensions={1}, use_global_device_ids=true | all-gather | bytes 10240 | tf_op jit(solution)/shard_map/all_gather | solution.py:78
  326.3 4.5 %collective-permute-start.16 = (f32[16,128]{1,0:T(8,128)S(1)}, f32[16,128]{1,0:T(8,128)S(1)}, u32[]{:S(2)}, u32[]{:S(2)}) collective-permute-start(f32[16,128]{1,0:T(8,128)S(1)} %get-tuple-element.74), channel_id=1, source_target_pairs={{0,4},{4,8},{8,12},{12,16},{16,20},{20,24},{24,28},{1,5},{5,9},{9,... | collective-permute-start | bytes 24584 | tf_op jit(solution)/shard_map/ppermute | solution.py:25
  332.6 1.3 collective-permute-start.19
  333.9 3.0 collective-permute-start.18
  337.1 1.3 collective-permute-start.11
  338.4 4.2 collective-permute-start.10
  342.6 1.6 fusion.120
  344.2 2.0 fusion.258
  346.2 5.1 %stack.206 = f32[8]{0:T(128)S(1)} concatenate(f32[1]{0:T(128)} %bitcast.80, f32[1]{0:T(128)} %bitcast.81, f32[1]{0:T(128)} %bitcast.82, f32[1]{0:T(128)} %bitcast.83, f32[1]{0:T(128)} %bitcast.84, f32[1]{0:T(128)} %bitcast.85, f32[1]{0:T(128)} %bitcast.86, f32[1]{0:T(128)} %bitcast.87), dimensions={0} | concatenate | bytes 64 | tf_op jit(solution)/shard_map/stack | solution.py:98
  352.0 5.1 %fusion.224 = f32[1,256,128]{2,1,0:T(8,128)S(1)} fusion(f32[]{:T(128)} %bitcast.95, f32[]{:T(128)} %bitcast.94, f32[]{:T(128)} %bitcast.93, f32[]{:T(128)} %bitcast.92, f32[]{:T(128)} %bitcast.91, f32[]{:T(128)} %bitcast.90, f32[]{:T(128)} %bitcast.89, f32[]{:T(128)} %bitcast.88, bf16[8,256,128]{2,1,0:T(8,128)(2,1)S(1)} %copy-done), kind=kLoop, calls=%fused_computation.294 | loop fusion | flops 753664 | bytes 655392 | tf_op jit(solution)/shard_map/add | solution.py:93
  357.1 5.1 %fusion.188 = f32[256,128]{1,0:T(8,128)S(1)} fusion(f32[]{:T(128)} %bitcast.95, f32[]{:T(128)} %bitcast.94, f32[]{:T(128)} %bitcast.93, f32[]{:T(128)} %bitcast.92, f32[]{:T(128)} %bitcast.91, f32[]{:T(128)} %bitcast.90, f32[]{:T(128)} %bitcast.89, f32[]{:T(128)} %bitcast.88, bf16[8,256,128]{2,1,0:T(8,128)(2,1)S(1)} %copy-done), kind=kLoop, calls=%fused_computation.258 | loop fusion | flops 753664 | bytes 655392 | tf_op jit(solution)/shard_map/add | solution.py:93
  363.7 30.5 %all-gather.5 = f32[8,32,16]{1,2,0:T(8,128)S(1)} all-gather(f32[1,32,16]{1,2,0:T(8,128)S(1)} %copy.70), channel_id=1, replica_groups=mesh['groups'=1,'along'=8,'across'=4] {'along'}, dimensions={0}, use_global_device_ids=true | all-gather | bytes 18432 | tf_op jit(solution)/shard_map/all_gather | solution.py:74
  395.6 4.5 %collective-permute-start.20 = (f32[16,128]{1,0:T(8,128)S(1)}, f32[16,128]{1,0:T(8,128)S(1)}, u32[]{:S(2)}, u32[]{:S(2)}) collective-permute-start(f32[16,128]{1,0:T(8,128)S(1)} %get-tuple-element.72), channel_id=1, source_target_pairs={{0,4},{4,8},{8,12},{12,16},{16,20},{20,24},{24,28},{1,5},{5,9},{9,... | collective-permute-start | bytes 24584 | tf_op jit(solution)/shard_map/ppermute | solution.py:25
  400.2 2.5 fusion.104
  402.7 2.0 convolution_add_fusion.3
  404.9 5.2 %all_gather.47 = f32[32,64]{0,1:T(8,128)S(1)} all-gather(f32[32,16]{0,1:T(8,128)S(1)} %fusion.278), channel_id=1, replica_groups=mesh['groups'=1,'along'=8,'across'=4] {'across'}, dimensions={1}, use_global_device_ids=true | all-gather | bytes 10240 | tf_op jit(solution)/shard_map/all_gather | solution.py:78
  410.2 1.3 collective-permute-start.23
  411.5 3.7 collective-permute-start.22
  416.9 2.5 fusion.130
  419.3 2.1 fusion.259
  421.4 5.1 %stack.215 = f32[8]{0:T(128)S(1)} concatenate(f32[1]{0:T(128)} %bitcast.97, f32[1]{0:T(128)} %bitcast.98, f32[1]{0:T(128)} %bitcast.99, f32[1]{0:T(128)} %bitcast.100, f32[1]{0:T(128)} %bitcast.101, f32[1]{0:T(128)} %bitcast.102, f32[1]{0:T(128)} %bitcast.103, f32[1]{0:T(128)} %bitcast.104), dimensions={0} | concatenate | bytes 64 | tf_op jit(solution)/shard_map/stack | solution.py:98
  (138 shorter events, 31.2 us)
Async XLA Ops:
  9.7 110.5 %collective-permute-start.1 = (f32[16,128]{1,0:T(8,128)S(1)}, f32[16,128]{1,0:T(8,128)S(1)}, u32[]{:S(2)}, u32[]{:S(2)}) collective-permute-start(f32[16,128]{1,0:T(8,128)S(1)} %get-tuple-element.81), channel_id=1, source_target_pairs={{4,0},{8,4},{12,8},{16,12},{20,16},{24,20},{28,24},{5,1},{9,5},{13... | collective-permute-start | bytes 24584 | tf_op jit(solution)/shard_map/ppermute | solution.py:27
  11.0 109.2 %collective-permute-start = (f32[16,128]{1,0:T(8,128)S(1)}, f32[16,128]{1,0:T(8,128)S(1)}, u32[]{:S(2)}, u32[]{:S(2)}) collective-permute-start(f32[16,128]{1,0:T(8,128)S(1)} %get-tuple-element.80), channel_id=1, source_target_pairs={{0,4},{4,8},{8,12},{12,16},{16,20},{20,24},{24,28},{1,5},{5,9},{9,... | collective-permute-start | bytes 24584 | tf_op jit(solution)/shard_map/ppermute | solution.py:25
  17.2 107.5 %collective-permute-start.12 = (f32[16,128]{1,0:T(8,128)S(1)}, f32[16,128]{1,0:T(8,128)S(1)}, u32[]{:S(2)}, u32[]{:S(2)}) collective-permute-start(f32[16,128]{1,0:T(8,128)S(1)} %get-tuple-element.83), channel_id=1, source_target_pairs={{0,4},{4,8},{8,12},{12,16},{16,20},{20,24},{24,28},{1,5},{5,9},{9,... | collective-permute-start | bytes 24584 | tf_op jit(solution)/shard_map/ppermute | solution.py:25
  22.0 102.7 %collective-permute-start.13 = (f32[16,128]{1,0:T(8,128)S(1)}, f32[16,128]{1,0:T(8,128)S(1)}, u32[]{:S(2)}, u32[]{:S(2)}) collective-permute-start(f32[16,128]{1,0:T(8,128)S(1)} %get-tuple-element.82), channel_id=1, source_target_pairs={{4,0},{8,4},{12,8},{16,12},{20,16},{24,20},{28,24},{5,1},{9,5},{13... | collective-permute-start | bytes 24584 | tf_op jit(solution)/shard_map/ppermute | solution.py:27
  36.0 74.6 %copy-start = (bf16[8,256,128]{2,1,0:T(8,128)(2,1)S(1)}, bf16[8,256,128]{2,1,0:T(8,128)(2,1)}, u32[]{:S(2)}) copy-start(bf16[8,256,128]{2,1,0:T(8,128)(2,1)} %param.8) | copy-start | bytes 1572868
  112.9 11.8 %copy-start.1 = (f32[256,128]{1,0:T(8,128)S(1)}, f32[256,128]{1,0:T(8,128)}, u32[]{:S(2)}) copy-start(f32[256,128]{1,0:T(8,128)} %param.9) | copy-start | bytes 393220
  120.3 10.6 %collective-permute-start.3 = (f32[288,16]{1,0:T(8,128)S(1)}, f32[288,16]{1,0:T(8,128)S(1)}, u32[]{:S(2)}, u32[]{:S(2)}) collective-permute-start(f32[288,16]{1,0:T(8,128)S(1)} %get-tuple-element.69), channel_id=1, source_target_pairs={{1,0},{2,1},{3,2},{5,4},{6,5},{7,6},{9,8},{10,9},{11,10},{13,12},{... | collective-permute-start | bytes 55304 | tf_op jit(solution)/shard_map/ppermute | solution.py:27
  121.6 9.3 %collective-permute-start.2 = (f32[288,16]{1,0:T(8,128)S(1)}, f32[288,16]{1,0:T(8,128)S(1)}, u32[]{:S(2)}, u32[]{:S(2)}) collective-permute-start(f32[288,16]{1,0:T(8,128)S(1)} %get-tuple-element.68), channel_id=1, source_target_pairs={{0,1},{1,2},{2,3},{4,5},{5,6},{6,7},{8,9},{9,10},{10,11},{12,13},{... | collective-permute-start | bytes 55304 | tf_op jit(solution)/shard_map/ppermute | solution.py:25
  124.8 76.0 %collective-permute-start.15 = (f32[288,16]{1,0:T(8,128)S(1)}, f32[288,16]{1,0:T(8,128)}, u32[]{:S(2)}, u32[]{:S(2)}) collective-permute-start(f32[288,16]{1,0:T(8,128)S(1)} %get-tuple-element.71), channel_id=1, source_target_pairs={{1,0},{2,1},{3,2},{5,4},{6,5},{7,6},{9,8},{10,9},{11,10},{13,12},{... | collective-permute-start | bytes 55304 | tf_op jit(solution)/shard_map/ppermute | solution.py:27
  126.1 74.7 %collective-permute-start.14 = (f32[288,16]{1,0:T(8,128)S(1)}, f32[288,16]{1,0:T(8,128)}, u32[]{:S(2)}, u32[]{:S(2)}) collective-permute-start(f32[288,16]{1,0:T(8,128)S(1)} %get-tuple-element.70), channel_id=1, source_target_pairs={{0,1},{1,2},{2,3},{4,5},{5,6},{6,7},{8,9},{9,10},{10,11},{12,13},{... | collective-permute-start | bytes 55304 | tf_op jit(solution)/shard_map/ppermute | solution.py:25
  188.0 6.1 %collective-permute-start.5 = (f32[16,128]{1,0:T(8,128)S(1)}, f32[16,128]{1,0:T(8,128)S(1)}, u32[]{:S(2)}, u32[]{:S(2)}) collective-permute-start(f32[16,128]{1,0:T(8,128)S(1)} %get-tuple-element.79), channel_id=1, source_target_pairs={{4,0},{8,4},{12,8},{16,12},{20,16},{24,20},{28,24},{5,1},{9,5},{13... | collective-permute-start | bytes 24584 | tf_op jit(solution)/shard_map/ppermute | solution.py:27
  189.2 5.9 %collective-permute-start.4 = (f32[16,128]{1,0:T(8,128)S(1)}, f32[16,128]{1,0:T(8,128)S(1)}, u32[]{:S(2)}, u32[]{:S(2)}) collective-permute-start(f32[16,128]{1,0:T(8,128)S(1)} %get-tuple-element.78), channel_id=1, source_target_pairs={{0,4},{4,8},{8,12},{12,16},{16,20},{20,24},{24,28},{1,5},{5,9},{9,... | collective-permute-start | bytes 24584 | tf_op jit(solution)/shard_map/ppermute | solution.py:25
  195.9 9.5 %collective-permute-start.7 = (f32[288,16]{1,0:T(8,128)}, f32[288,16]{1,0:T(8,128)}, u32[]{:S(2)}, u32[]{:S(2)}) collective-permute-start(f32[288,16]{1,0:T(8,128)} %get-tuple-element.67), channel_id=1, source_target_pairs={{1,0},{2,1},{3,2},{5,4},{6,5},{7,6},{9,8},{10,9},{11,10},{13,12},{... | collective-permute-start | bytes 55304 | tf_op jit(solution)/shard_map/ppermute | solution.py:27
  197.2 8.2 %collective-permute-start.6 = (f32[288,16]{1,0:T(8,128)S(1)}, f32[288,16]{1,0:T(8,128)}, u32[]{:S(2)}, u32[]{:S(2)}) collective-permute-start(f32[288,16]{1,0:T(8,128)S(1)} %get-tuple-element.66), channel_id=1, source_target_pairs={{0,1},{1,2},{2,3},{4,5},{5,6},{6,7},{8,9},{9,10},{10,11},{12,13},{... | collective-permute-start | bytes 55304 | tf_op jit(solution)/shard_map/ppermute | solution.py:25
  205.4 4.0 copy-start.2
  205.4 4.0 copy-start.4
  281.7 55.3 %collective-permute-start.9 = (f32[16,128]{1,0:T(8,128)S(1)}, f32[16,128]{1,0:T(8,128)S(1)}, u32[]{:S(2)}, u32[]{:S(2)}) collective-permute-start(f32[16,128]{1,0:T(8,128)S(1)} %get-tuple-element.77), channel_id=1, source_target_pairs={{4,0},{8,4},{12,8},{16,12},{20,16},{24,20},{28,24},{5,1},{9,5},{13... | collective-permute-start | bytes 24584 | tf_op jit(solution)/shard_map/ppermute | solution.py:27
  283.0 54.0 %collective-permute-start.8 = (f32[16,128]{1,0:T(8,128)S(1)}, f32[16,128]{1,0:T(8,128)S(1)}, u32[]{:S(2)}, u32[]{:S(2)}) collective-permute-start(f32[16,128]{1,0:T(8,128)S(1)} %get-tuple-element.76), channel_id=1, source_target_pairs={{0,4},{4,8},{8,12},{12,16},{16,20},{20,24},{24,28},{1,5},{5,9},{9,... | collective-permute-start | bytes 24584 | tf_op jit(solution)/shard_map/ppermute | solution.py:25
  325.0 7.5 %collective-permute-start.17 = (f32[16,128]{1,0:T(8,128)S(1)}, f32[16,128]{1,0:T(8,128)S(1)}, u32[]{:S(2)}, u32[]{:S(2)}) collective-permute-start(f32[16,128]{1,0:T(8,128)S(1)} %get-tuple-element.75), channel_id=1, source_target_pairs={{4,0},{8,4},{12,8},{16,12},{20,16},{24,20},{28,24},{5,1},{9,5},{13... | collective-permute-start | bytes 24584 | tf_op jit(solution)/shard_map/ppermute | solution.py:27
  326.3 6.2 %collective-permute-start.16 = (f32[16,128]{1,0:T(8,128)S(1)}, f32[16,128]{1,0:T(8,128)S(1)}, u32[]{:S(2)}, u32[]{:S(2)}) collective-permute-start(f32[16,128]{1,0:T(8,128)S(1)} %get-tuple-element.74), channel_id=1, source_target_pairs={{0,4},{4,8},{8,12},{12,16},{16,20},{20,24},{24,28},{1,5},{5,9},{9,... | collective-permute-start | bytes 24584 | tf_op jit(solution)/shard_map/ppermute | solution.py:25
  332.6 10.0 %collective-permute-start.19 = (f32[288,16]{1,0:T(8,128)S(1)}, f32[288,16]{1,0:T(8,128)S(1)}, u32[]{:S(2)}, u32[]{:S(2)}) collective-permute-start(f32[288,16]{1,0:T(8,128)S(1)} %get-tuple-element.63), channel_id=1, source_target_pairs={{1,0},{2,1},{3,2},{5,4},{6,5},{7,6},{9,8},{10,9},{11,10},{13,12},{... | collective-permute-start | bytes 55304 | tf_op jit(solution)/shard_map/ppermute | solution.py:27
  333.9 8.7 %collective-permute-start.18 = (f32[288,16]{1,0:T(8,128)S(1)}, f32[288,16]{1,0:T(8,128)S(1)}, u32[]{:S(2)}, u32[]{:S(2)}) collective-permute-start(f32[288,16]{1,0:T(8,128)S(1)} %get-tuple-element.62), channel_id=1, source_target_pairs={{0,1},{1,2},{2,3},{4,5},{5,6},{6,7},{8,9},{9,10},{10,11},{12,13},{... | collective-permute-start | bytes 55304 | tf_op jit(solution)/shard_map/ppermute | solution.py:25
  337.1 63.0 %collective-permute-start.11 = (f32[288,16]{1,0:T(8,128)S(1)}, f32[288,16]{1,0:T(8,128)}, u32[]{:S(2)}, u32[]{:S(2)}) collective-permute-start(f32[288,16]{1,0:T(8,128)S(1)} %get-tuple-element.65), channel_id=1, source_target_pairs={{1,0},{2,1},{3,2},{5,4},{6,5},{7,6},{9,8},{10,9},{11,10},{13,12},{... | collective-permute-start | bytes 55304 | tf_op jit(solution)/shard_map/ppermute | solution.py:27
  338.4 61.7 %collective-permute-start.10 = (f32[288,16]{1,0:T(8,128)S(1)}, f32[288,16]{1,0:T(8,128)}, u32[]{:S(2)}, u32[]{:S(2)}) collective-permute-start(f32[288,16]{1,0:T(8,128)S(1)} %get-tuple-element.64), channel_id=1, source_target_pairs={{0,1},{1,2},{2,3},{4,5},{5,6},{6,7},{8,9},{9,10},{10,11},{12,13},{... | collective-permute-start | bytes 55304 | tf_op jit(solution)/shard_map/ppermute | solution.py:25
  394.3 15.8 %collective-permute-start.21 = (f32[16,128]{1,0:T(8,128)S(1)}, f32[16,128]{1,0:T(8,128)S(1)}, u32[]{:S(2)}, u32[]{:S(2)}) collective-permute-start(f32[16,128]{1,0:T(8,128)S(1)} %get-tuple-element.73), channel_id=1, source_target_pairs={{4,0},{8,4},{12,8},{16,12},{20,16},{24,20},{28,24},{5,1},{9,5},{13... | collective-permute-start | bytes 24584 | tf_op jit(solution)/shard_map/ppermute | solution.py:27
  395.6 14.5 %collective-permute-start.20 = (f32[16,128]{1,0:T(8,128)S(1)}, f32[16,128]{1,0:T(8,128)S(1)}, u32[]{:S(2)}, u32[]{:S(2)}) collective-permute-start(f32[16,128]{1,0:T(8,128)S(1)} %get-tuple-element.72), channel_id=1, source_target_pairs={{0,4},{4,8},{8,12},{12,16},{16,20},{20,24},{24,28},{1,5},{5,9},{9,... | collective-permute-start | bytes 24584 | tf_op jit(solution)/shard_map/ppermute | solution.py:25
  410.2 6.6 %collective-permute-start.23 = (f32[288,16]{1,0:T(8,128)S(1)}, f32[288,16]{1,0:T(8,128)S(1)}, u32[]{:S(2)}, u32[]{:S(2)}) collective-permute-start(f32[288,16]{1,0:T(8,128)S(1)} %get-tuple-element.61), channel_id=1, source_target_pairs={{1,0},{2,1},{3,2},{5,4},{6,5},{7,6},{9,8},{10,9},{11,10},{13,12},{... | collective-permute-start | bytes 55304 | tf_op jit(solution)/shard_map/ppermute | solution.py:27
  411.5 5.3 %collective-permute-start.22 = (f32[288,16]{1,0:T(8,128)S(1)}, f32[288,16]{1,0:T(8,128)}, u32[]{:S(2)}, u32[]{:S(2)}) collective-permute-start(f32[288,16]{1,0:T(8,128)S(1)} %get-tuple-element.60), channel_id=1, source_target_pairs={{0,1},{1,2},{2,3},{4,5},{5,6},{6,7},{8,9},{9,10},{10,11},{12,13},{... | collective-permute-start | bytes 55304 | tf_op jit(solution)/shard_map/ppermute | solution.py:25
  416.8 9.6 %copy-start.3 = (s32[1,1,512]{2,1,0:T(1,128)S(1)}, s32[1,1,512]{2,1,0:T(1,128)}, u32[]{:S(2)}) copy-start(s32[1,1,512]{2,1,0:T(1,128)} %param.6) | copy-start | bytes 6148
where the time goes:
time: 431 us; the launch traced here: 427 us
  blocking collectives  216 us (50%)
  starting transfers between devices  66.4 us (15%)
  other arithmetic  59.5 us (14%)
  local copies, waits for them, and re-layouts  53.8 us (12%)
  matrix products  28.7 us (7%)
    all_gather x6, blocking collectives, blur_back(): piece = lax.all_gather(coarse, 'along', axis=0, tiled=True)  185 us
    add x10, other arithmetic, dose_map(): total = total + coef[kind] * dose_weights[kind].astype(jnp.float32)  53 us
    ppermute x12, starting transfers between devices, extended(): lax.ppermute(tail, axis, [(i, (i + 1) % count) for i in range(ends)])  50.9 us
    all_gather x6, blocking collectives, blur_back(): piece = lax.all_gather(along_blur, 'across', axis=1, tiled=True)  31.2 us
    another operation x5, local copies, waits for them, and re-layouts, weighted(): jnp.stack([jnp.sum(dose_weights[kind].astype(jnp.float32) * field) for ki...  25.3 us
    ppermute x12, starting transfers between devices, extended(): lax.ppermute(head, axis, [((i + 1) % count, i) for i in range(ends)])  15.5 us
    dot_general x6, matrix products, blur_fine(): middle = jnp.dot(band_rows, padded, precision=exact)  14 us
    dot_general x6, matrix products, blur_fine(): return jnp.dot(middle, band_cols.T, precision=exact)  11.5 us
  transfers between devices with their start and end apart: 24, of which 1 were waited for; matrix products, arithmetic and copies ran while one was open for 19% of the time, Pallas kernels for 0%

commit v1 on v0

v1 whole, which is shorter than its diff:
```python
import functools
import math

import jax
import jax.numpy as jnp
import numpy as np
from jax import lax
from jax.experimental import pallas as pl
from jax.experimental.pallas import tpu as pltpu
from jax.sharding import PartitionSpec as P

H = 16
LANES = 128
BLOCK = 8
sigma_fine = 3.75
sigma_back = 156.25
back_ratio = 0.7
FIELDS = (2, 1, 2, 1)
reach = np.arange(-H, H + 1).astype(np.float64)
fine_norm = float(np.sum(np.exp(-reach * reach / (2.0 * sigma_fine * sigma_fine))))


def fine_weight(distance):
    d = distance.astype(jnp.float32)
    return jnp.where(
        jnp.abs(distance) <= H, jnp.exp(-d * d / (2.0 * sigma_fine * sigma_fine)) / fine_norm, 0.0
    )


def back_weight(distance, factor=1.0):
    d = distance.astype(jnp.float32)
    return jnp.exp(-d * d / (2.0 * sigma_back * sigma_back)) * (
        factor / (math.sqrt(2.0 * math.pi) * sigma_back)
    )


def iota(shape, dim):
    return lax.broadcasted_iota(jnp.int32, shape, dim)


def halves(value):
    high = value.astype(jnp.bfloat16)
    return high, (value - high.astype(jnp.float32)).astype(jnp.bfloat16)


def mm(a, b):
    return jnp.dot(a, b, preferred_element_type=jnp.float32)


def dot3(a, b):
    return mm(a[0], b[0]) + (mm(a[0], b[1]) + mm(a[1], b[0]))


def kernel(na, nc, *refs):
    doses_ref, type_ref, count_ref, w_ref, cot_ref, out_ref, grad_ref = refs[:7]
    (
        wf, fld, cols_h, cols_l, side_h, side_l, rows_h, rows_l, edge_h, edge_l,
        along_h, along_l, across_h, across_l,
    ) = refs[7:21]
    rounds = [refs[21 + 8 * t : 29 + 8 * t] for t in range(4)]
    local_sems, send_sems, recv_sems = refs[53:56]
    kinds, row_count, col_count = w_ref.shape
    coarse_rows = row_count // BLOCK
    coarse_cols = col_count // BLOCK
    groups = LANES // coarse_cols
    packed = coarse_rows // groups
    ia = lax.axis_index("along")
    ic = lax.axis_index("across")
    up, down = lax.rem(ia + na - 1, na), lax.rem(ia + 1, na)
    left, right = lax.rem(ic + nc - 1, nc), lax.rem(ic + 1, nc)
    along_peers = [lax.rem(ia + o, na) for o in range(1, na)]
    across_peers = [lax.rem(ic + o, nc) for o in range(1, nc)]

    barrier = pltpu.get_barrier_semaphore()
    greeted = (
        [{"along": a} for a in along_peers]
        + [{"across": c} for c in across_peers]
        + [{"along": a, "across": c} for a in (up, down) for c in (left, right)]
    )
    for device in greeted:
        pl.semaphore_signal(barrier, inc=1, device_id=device, device_id_type=pl.DeviceIdType.MESH)

    lane_group = iota((groups, LANES), 1) // coarse_cols
    own_group = lane_group == iota((groups, LANES), 0)
    pool = jnp.where(
        iota((col_count, LANES), 0) // BLOCK == iota((col_count, LANES), 1) % coarse_cols,
        1.0 / (BLOCK * BLOCK),
        0.0,
    ).astype(jnp.bfloat16)
    repeat = jnp.where(
        iota((LANES, LANES), 0) % coarse_cols == iota((LANES, LANES), 1) % coarse_cols, 1.0, 0.0
    ).astype(jnp.bfloat16)

    def dose_map(coef):
        total = coef[0:1] * wf[0]
        for kind in range(1, kinds):
            total = total + coef[kind : kind + 1] * wf[kind]
        return total

    def weighted(field):
        sums = []
        for kind in range(kinds):
            value = wf[kind] if field is None else wf[kind] * field
            part = value.reshape(row_count // 8, 8, col_count).sum(axis=0)
            sums.append(jnp.sum(part, axis=0, keepdims=True))
        return jnp.broadcast_to(
            jnp.sum(jnp.concatenate(sums, axis=0), axis=1, keepdims=True), (kinds, col_count)
        )

    def remote(src, dst, t, which, device):
        pltpu.make_async_remote_copy(
            src_ref=src,
            dst_ref=dst,
            send_sem=send_sems.at[t, which],
            recv_sem=recv_sems.at[t, which],
            device_id=device,
            device_id_type=pl.DeviceIdType.MESH,
        ).start()

    def wait_for(ref, sem):
        pltpu.make_async_copy(ref, ref, sem).wait()

    def send_first(t, fields):
        ca, cb, strip, side, ga, gb, halo_rows, halo_cols = rounds[t]
        for f, field in enumerate(fields):
            high, low = halves(field)
            pooled = mm(high, pool) + mm(low, pool)
            for r in range(packed):
                total = None
                for g in range(groups):
                    start = (r * groups + g) * BLOCK
                    term = jnp.where(lane_group == g, pooled[start : start + BLOCK], 0.0)
                    total = term if total is None else total + term
                ca[packed * f + r : packed * f + r + 1] = jnp.sum(total, axis=0, keepdims=True)
        pltpu.make_async_copy(ca, ga.at[ia], recv_sems.at[t, 0]).start()
        for peer in along_peers:
            remote(ca, ga.at[ia], t, 0, {"along": peer})
        for f, field in enumerate(fields):
            strip[0, f] = field[:H]
            strip[1, f] = field[row_count - H :]
            fld[f] = field
        for slot, c in ((1, None), (2, left), (0, right)):
            for tb, a in ((0, up), (1, down)):
                device = {"along": a} if c is None else {"along": a, "across": c}
                remote(strip.at[tb], halo_rows.at[slot, 1 - tb], t, 1, device)
        for f, field in enumerate(fields):
            turned = field.T
            side[0, f] = turned[:H]
            side[1, f] = turned[col_count - H :]
        remote(side.at[0], halo_cols.at[1], t, 2, {"across": left})
        remote(side.at[1], halo_cols.at[0], t, 2, {"across": right})

    def spread(row):
        return jnp.where(own_group, jnp.broadcast_to(row, (groups, LANES)), 0.0)

    def finish(t):
        ca, cb, strip, side, ga, gb, halo_rows, halo_cols = rounds[t]
        count = FIELDS[t]
        wait_for(ga, recv_sems.at[t, 0])
        theirs = jnp.concatenate(
            [
                jnp.concatenate(
                    [
                        spread(ga[a, packed * f + r : packed * f + r + 1])
                        for a in range(na)
                        for r in range(packed)
                    ],
                    axis=0,
                )
                for f in range(count)
            ],
            axis=1,
        )
        blurred = dot3((along_h[...], along_l[...]), halves(theirs))
        blurred = jnp.concatenate(
            [blurred[:, f * LANES : (f + 1) * LANES] for f in range(count)], axis=0
        )
        high, low = halves(blurred)
        blurred = mm(high, repeat) + mm(low, repeat)
        for i in range(packed * count):
            part = jnp.where(own_group, blurred[i * groups : (i + 1) * groups], 0.0)
            cb[i : i + 1] = jnp.sum(part, axis=0, keepdims=True)
        pltpu.make_async_copy(cb, gb.at[ic], recv_sems.at[t, 3]).start()
        for peer in across_peers:
            remote(cb, gb.at[ic], t, 3, {"across": peer})

        wait_for(halo_rows, recv_sems.at[t, 1])
        wait_for(halo_cols, recv_sems.at[t, 2])
        middles, edges = [], []
        cols = (cols_h[...], cols_l[...])
        centre = (cols_h[col_count : 2 * col_count], cols_l[col_count : 2 * col_count])
        for f in range(count):
            beside = jnp.concatenate([halo_cols[0, f], halo_cols[1, f]], axis=0).T
            middles.append(
                dot3(halves(fld[f]), centre) + dot3(halves(beside), (side_h[...], side_l[...]))
            )
            outer = jnp.concatenate(
                [
                    jnp.concatenate([halo_rows[s, 0, f], halo_rows[s, 1, f]], axis=0)
                    for s in range(3)
                ],
                axis=1,
            )
            edges.append(dot3(halves(outer), cols))
        middle = jnp.concatenate(middles, axis=1)
        edge = jnp.concatenate(edges, axis=1)
        fine = dot3((rows_h[...], rows_l[...]), halves(middle)) + dot3(
            (edge_h[...], edge_l[...]), halves(edge)
        )

        wait_for(gb, recv_sems.at[t, 3])
        both = jnp.concatenate(
            [
                jnp.concatenate([spread(gb[c, i : i + 1]) for c in range(nc)], axis=1)
                for i in range(packed * count)
            ],
            axis=0,
        )
        back = dot3(halves(both), (across_h[...], across_l[...]))
        results = []
        for f in range(count):
            wide = jnp.concatenate(
                [
                    jnp.broadcast_to(back[p : p + 1], (BLOCK, col_count))
                    for p in range(f * coarse_rows, (f + 1) * coarse_rows)
                ],
                axis=0,
            )
            results.append(fine[:, f * col_count : (f + 1) * col_count] + wide)
        return results

    shots = doses_ref.shape[-1]
    share = kinds / shots
    live = (iota((1, shots), 1) < count_ref[...]).astype(jnp.float32)
    chosen = (type_ref[0] == iota((kinds, shots), 0)).astype(jnp.float32)
    coef0 = share * jnp.broadcast_to(
        jnp.sum(chosen * (live * doses_ref[0]), axis=1, keepdims=True), (kinds, col_count)
    )
    for kind in range(kinds):
        wf[kind] = w_ref[kind].astype(jnp.float32)
    first = dose_map(coef0)

    pl.semaphore_wait(barrier, len(greeted))
    send_first(0, [first, cot_ref[...]])

    def keep(refs_pair, value):
        refs_pair[0][...], refs_pair[1][...] = halves(value)

    shape = (coarse_rows, na * coarse_rows)
    keep((along_h, along_l), back_weight(ia * coarse_rows + iota(shape, 0) - iota(shape, 1)))
    shape = (col_count, col_count)
    gap = iota(shape, 1) - iota(shape, 0)
    lefts = jnp.where(ic > 0, fine_weight(gap + col_count), 0.0)
    rights = jnp.where(ic < nc - 1, fine_weight(gap - col_count), 0.0)
    keep((cols_h, cols_l), jnp.concatenate([lefts, fine_weight(gap), rights], axis=0))
    keep((side_h, side_l), jnp.concatenate([lefts[col_count - H :], rights[:H]], axis=0))
    shape = (row_count, row_count)
    keep((rows_h, rows_l), fine_weight(iota(shape, 0) - iota(shape, 1)))
    shape = (row_count, 2 * H)
    spot = iota(shape, 1)
    above = jnp.where(ia > 0, fine_weight(iota(shape, 0) - (spot - H)), 0.0)
    below = jnp.where(ia < na - 1, fine_weight(iota(shape, 0) - (spot - H + row_count)), 0.0)
    keep((edge_h, edge_l), jnp.where(spot < H, above, below))
    shape = (nc * LANES, col_count)
    source = iota(shape, 0) // LANES * coarse_cols + iota(shape, 0) % coarse_cols
    keep(
        (across_h, across_l),
        back_weight(source - (ic * coarse_cols + iota(shape, 1) // BLOCK), back_ratio),
    )
    totals = weighted(None)

    field, pulled = finish(0)
    ratio0 = weighted(field) / totals
    coef1 = coef0 / ratio0
    send_first(1, [dose_map(coef1)])
    grad2 = weighted(pulled)

    (field,) = finish(1)
    ratio1 = weighted(field) / totals
    coef2 = coef1 / ratio1
    grad_ratio1 = -grad2 * coef2 / ratio1
    send_first(2, [dose_map(coef2), dose_map(grad_ratio1 / totals)])

    exposure, field = finish(2)
    grad1 = grad2 / ratio1 + weighted(field)
    grad_ratio0 = -grad1 * coef1 / ratio0
    send_first(3, [dose_map(grad_ratio0 / totals)])
    out_ref[...] = exposure

    (field,) = finish(3)
    grad0 = grad1 / ratio0 + weighted(field)
    grad_ref[0] = live * share * jnp.sum(chosen * grad0[:, 0:1], axis=0, keepdims=True)

    for t in range(4):
        ca, cb, strip, side, ga, gb, halo_rows, halo_cols = rounds[t]
        wait_for(ga.at[: na - 1], send_sems.at[t, 0])
        wait_for(halo_rows, send_sems.at[t, 1])
        wait_for(halo_cols, send_sems.at[t, 2])
        wait_for(gb.at[: nc - 1], send_sems.at[t, 3])


def shards(na, nc, doses, shot_type, shot_count, dose_weights, cotangent):
    kinds, rows, cols = dose_weights.shape
    f32, bf16 = jnp.float32, jnp.bfloat16
    coarse_rows = rows // BLOCK
    packed = coarse_rows * (cols // BLOCK) // LANES

    def pair(*shape):
        return [pltpu.VMEM(shape, bf16), pltpu.VMEM(shape, bf16)]

    scratch = [pltpu.VMEM((kinds, rows, cols), f32), pltpu.VMEM((2, rows, cols), f32)]
    scratch += pair(3 * cols, cols) + pair(2 * H, cols) + pair(rows, rows) + pair(rows, 2 * H)
    scratch += pair(coarse_rows, na * coarse_rows) + pair(nc * LANES, cols)
    for count in FIELDS:
        scratch += [
            pltpu.VMEM((packed * count, LANES), f32),
            pltpu.VMEM((packed * count, LANES), f32),
            pltpu.VMEM((2, count, H, cols), f32),
            pltpu.VMEM((2, count, H, rows), f32),
            pltpu.VMEM((na, packed * count, LANES), f32),
            pltpu.VMEM((nc, packed * count, LANES), f32),
            pltpu.VMEM((3, 2, count, H, cols), f32),
            pltpu.VMEM((2, count, H, rows), f32),
        ]
    scratch += [
        pltpu.SemaphoreType.DMA((4,)),
        pltpu.SemaphoreType.DMA((4, 4)),
        pltpu.SemaphoreType.DMA((4, 4)),
    ]
    return pl.pallas_call(
        functools.partial(kernel, na, nc),
        out_shape=(
            jax.ShapeDtypeStruct(cotangent.shape, f32),
            jax.ShapeDtypeStruct(doses.shape, f32),
        ),
        in_specs=[pl.BlockSpec(memory_space=pltpu.VMEM)] * 5,
        out_specs=(pl.BlockSpec(memory_space=pltpu.VMEM),) * 2,
        scratch_shapes=scratch,
        compiler_params=pltpu.CompilerParams(
            collective_id=0, has_side_effects=True, vmem_limit_bytes=32 * 1024 * 1024
        ),
    )(doses, shot_type, shot_count, dose_weights, cotangent)


def solution(mesh):
    in_specs = (
        P(("groups", "along"), "across", None),
        P(("groups", "along"), "across", None),
        P(("groups", "along"), "across"),
        P(None, ("groups", "along"), "across"),
        P(("groups", "along"), "across"),
    )
    out_specs = (P(("groups", "along"), "across"), P(("groups", "along"), "across", None))
    run = functools.partial(shards, mesh.shape["along"], mesh.shape["across"])
    return jax.shard_map(run, mesh=mesh, in_specs=in_specs, out_specs=out_specs, check_vma=False)
```

time: 431 us -> 43.8 us (0.10)
  blocking collectives: 216 us -> 0 us
  starting transfers between devices: 66.4 us -> 0 us
  other arithmetic: 59.5 us -> 0 us
  local copies, waits for them, and re-layouts: 53.8 us -> 4.54 us
  Pallas kernels: 0 us -> 37.8 us
  matrix products: 28.7 us -> 0 us
    all_gather x12 -> x0, blocking collectives: 216 us -> none  [the longest x6 185 us: blur_back(): piece = lax.all_gather(coarse, 'along', axis=0, tiled=True)]
    ppermute x24 -> x0, starting transfers between devices: 66.4 us -> none  [the longest x12 50.9 us: extended(): lax.ppermute(tail, axis, [(i, (i + 1) % count) for i in range(ends)])]
    add x10 -> x0, other arithmetic: 53 us -> none  [dose_map(): total = total + coef[kind] * dose_weights[kind].astype(jnp.float32)]
    pallas_call x0 -> x1, Pallas kernels: none -> 37.8 us  [shards(): pl.pallas_call(functools.partial(kernel, na, nc), out_shape=(jax.ShapeDty...]
    another operation x6 -> x0, local copies, waits for them, and re-layouts: 30.3 us -> none  [the longest x5 25.3 us: weighted(): jnp.stack([jnp.sum(dose_weights[kind].astype(jnp.float32) * field) for ki...]
    dot_general x25 -> x0, matrix products: 28.7 us -> none  [the longest x6 14 us: blur_fine(): middle = jnp.dot(band_rows, padded, precision=exact)]
    mul x12 -> x0, local copies, waits for them, and re-layouts: 7.25 us -> none  [operator_apply(): return blur_fine(field) + back_ratio * blur_back(field)]
    add x5 -> x0, local copies, waits for them, and re-layouts: 7.01 us -> none  [dose_map(): total = total + coef[kind] * dose_weights[kind].astype(jnp.float32)]
  transfers between devices with their start and end apart: 24 -> 0, of which waited for: 1 -> 0; matrix products, arithmetic and copies ran while one was open for 19% -> 0% of each run, Pallas kernels for 0% -> 0%
where the time goes in v1:
time: 43.8 us; the launch traced here: 43.6 us
  Pallas kernels  37.8 us (86%)
  local copies, waits for them, and re-layouts  4.54 us (10%)
  between operations  1.3 us (3%)
    pallas_call x1, Pallas kernels, shards(): pl.pallas_call(functools.partial(kernel, na, nc), out_shape=(jax.ShapeDty...  37.8 us
    unnamed x10, local copies, waits for them, and re-layouts  4.54 us

profile of v1, /device:TPU:0, one launch (start us, length us, event | category | flops | bytes accessed | tf_op | source)
XLA Modules:
  0.0 43.6 jit_solution(12193807393742728408)
XLA Ops:
  1.3 0.0 copy-start
  1.3 1.0 %copy-done = bf16[8,256,128]{2,1,0:T(8,128)(2,1)S(1)} copy-done((bf16[8,256,128]{2,1,0:T(8,128)(2,1)S(1)}, bf16[8,256,128]{2,1,0:T(8,128)(2,1)}, u32[]{:S(2)}) %copy-start) | copy-done | bytes 524312
  2.3 0.0 copy-start.1
  2.3 0.9 %copy-done.1 = f32[256,128]{1,0:T(8,128)S(1)} copy-done((f32[256,128]{1,0:T(8,128)S(1)}, f32[256,128]{1,0:T(8,128)}, u32[]{:S(2)}) %copy-start.1) | copy-done | bytes 131096
  3.2 0.0 copy-start.2
  3.2 0.7 %copy-done.2 = f32[1,1,512]{2,1,0:T(1,128)S(1)} copy-done((f32[1,1,512]{2,1,0:T(1,128)S(1)}, f32[1,1,512]{2,1,0:T(1,128)}, u32[]{:S(2)}) %copy-start.2) | copy-done | bytes 2072
  3.9 0.0 copy-start.3
  3.9 0.7 %copy-done.3 = s32[1,1,512]{2,1,0:T(1,128)S(1)} copy-done((s32[1,1,512]{2,1,0:T(1,128)S(1)}, s32[1,1,512]{2,1,0:T(1,128)}, u32[]{:S(2)}) %copy-start.3) | copy-done | bytes 2072
  4.6 37.8 %shard_map.68 = (f32[256,128]{1,0:T(8,128)S(1)}, f32[1,1,512]{2,1,0:T(1,128)S(1)}) custom-call(f32[1,1,512]{2,1,0:T(1,128)S(1)} %copy-done.2, s32[1,1,512]{2,1,0:T(1,128)S(1)} %copy-done.3, s32[1,1]{1,0:T(1,128)S(6)} %copy.9.refs_2_, bf16[8,256,128]{2,1,0:T(8,128)(2,1)S(1)} %copy-done, f32[256,128]{1,0:T(8,128)S(1)} %copy-done.1), custom_call_target="tpu_custom_call" | custom-call | tf_op jit(solution)/shard_map/pallas_call | solution.py:330
  42.4 0.7 %copy.10 = f32[256,128]{1,0:T(8,128)} copy(f32[256,128]{1,0:T(8,128)S(1)} %get-tuple-element.4) | data formatting | bytes 262144
  43.0 0.6 %copy.11 = f32[1,1,512]{2,1,0:T(1,128)} copy(f32[1,1,512]{2,1,0:T(1,128)S(1)} %get-tuple-element.5) | data formatting | bytes 4096
Async XLA Ops:
  1.3 1.0 %copy-start = (bf16[8,256,128]{2,1,0:T(8,128)(2,1)S(1)}, bf16[8,256,128]{2,1,0:T(8,128)(2,1)}, u32[]{:S(2)}) copy-start(bf16[8,256,128]{2,1,0:T(8,128)(2,1)} %refs_3_.1) | copy-start | bytes 1572868
  2.3 0.9 %copy-start.1 = (f32[256,128]{1,0:T(8,128)S(1)}, f32[256,128]{1,0:T(8,128)}, u32[]{:S(2)}) copy-start(f32[256,128]{1,0:T(8,128)} %refs_4_.1) | copy-start | bytes 393220
  3.2 0.7 %copy-start.2 = (f32[1,1,512]{2,1,0:T(1,128)S(1)}, f32[1,1,512]{2,1,0:T(1,128)}, u32[]{:S(2)}) copy-start(f32[1,1,512]{2,1,0:T(1,128)} %refs_0_.1) | copy-start | bytes 6148
  3.9 0.7 %copy-start.3 = (s32[1,1,512]{2,1,0:T(1,128)S(1)}, s32[1,1,512]{2,1,0:T(1,128)}, u32[]{:S(2)}) copy-start(s32[1,1,512]{2,1,0:T(1,128)} %refs_1_.1) | copy-start | bytes 6148

commit v2 on v1

v2 whole, which is shorter than its diff:
```python
import functools
import math

import jax
import jax.numpy as jnp
import numpy as np
from jax import lax
from jax.experimental import pallas as pl
from jax.experimental.pallas import tpu as pltpu
from jax.sharding import PartitionSpec as P

H = 16
LANES = 128
BLOCK = 8
sigma_fine = 3.75
sigma_back = 156.25
back_ratio = 0.7
JOBS = 6
COTANGENT, EXPOSURE = 4, 5
reach = np.arange(-H, H + 1).astype(np.float64)
fine_norm = float(np.sum(np.exp(-reach * reach / (2.0 * sigma_fine * sigma_fine))))


def fine_weight(distance):
    d = distance.astype(jnp.float32)
    return jnp.where(
        jnp.abs(distance) <= H, jnp.exp(-d * d / (2.0 * sigma_fine * sigma_fine)) / fine_norm, 0.0
    )


def back_weight(distance, factor=1.0):
    d = distance.astype(jnp.float32)
    return jnp.exp(-d * d / (2.0 * sigma_back * sigma_back)) * (
        factor / (math.sqrt(2.0 * math.pi) * sigma_back)
    )


def iota(shape, dim):
    return lax.broadcasted_iota(jnp.int32, shape, dim)


def halves(value):
    high = value.astype(jnp.bfloat16)
    return high, (value - high.astype(jnp.float32)).astype(jnp.bfloat16)


def mm(a, b):
    return jnp.dot(a, b, preferred_element_type=jnp.float32)


def dot3(a, b):
    return mm(a[0], b[0]) + (mm(a[0], b[1]) + mm(a[1], b[0]))


def kernel(na, nc, *refs):
    doses_ref, type_ref, count_ref, w_ref, cot_ref, out_ref, grad_ref = refs[:7]
    (
        wf, fld, fine, cols_h, cols_l, side3, rows_h, rows_l, edge3, along3, across_h, across_l,
    ) = refs[7:19]
    jobs = [refs[19 + 6 * t : 25 + 6 * t] for t in range(JOBS)]
    send_sems, recv_sems = refs[19 + 6 * JOBS :]
    kinds, row_count, col_count = w_ref.shape
    coarse_rows = row_count // BLOCK
    coarse_cols = col_count // BLOCK
    groups = LANES // coarse_cols
    packed = coarse_rows // groups
    ia = lax.axis_index("along")
    ic = lax.axis_index("across")
    along_at = [lax.rem(ia + o, na) for o in range(na)]
    across_at = [lax.rem(ic + o, nc) for o in range(nc)]
    up, down = along_at[na - 1], along_at[1]
    left, right = across_at[nc - 1], across_at[1]
    offsets = sorted(range(na), key=lambda o: -min(o, na - o))
    peers = [
        {"along": along_at[oa], "across": across_at[oc]}
        for oa in offsets
        for oc in range(nc)
        if oa or oc
    ]

    barrier = pltpu.get_barrier_semaphore()
    for device in peers:
        pl.semaphore_signal(barrier, inc=1, device_id=device, device_id_type=pl.DeviceIdType.MESH)

    lane_group = iota((groups, LANES), 1) // coarse_cols
    pool = jnp.where(
        iota((col_count, LANES), 0) // BLOCK == iota((col_count, LANES), 1) % coarse_cols,
        1.0 / (BLOCK * BLOCK),
        0.0,
    ).astype(jnp.bfloat16)

    def dose_map(coef):
        total = coef[0:1] * wf[0]
        for kind in range(1, kinds):
            total = total + coef[kind : kind + 1] * wf[kind]
        return total

    def weighted(field):
        sums = []
        for kind in range(kinds):
            value = wf[kind] if field is None else wf[kind] * field
            part = value.reshape(row_count // 8, 8, col_count).sum(axis=0)
            sums.append(jnp.sum(part, axis=0, keepdims=True))
        return jnp.broadcast_to(
            jnp.sum(jnp.concatenate(sums, axis=0), axis=1, keepdims=True), (kinds, col_count)
        )

    def remote(src, dst, t, which, device):
        pltpu.make_async_remote_copy(
            src_ref=src,
            dst_ref=dst,
            send_sem=send_sems.at[t, which],
            recv_sem=recv_sems.at[t, which],
            device_id=device,
            device_id_type=pl.DeviceIdType.MESH,
        ).start()

    def wait_for(ref, sem):
        pltpu.make_async_copy(ref, ref, sem).wait()

    mine = ia * nc + ic

    def send(t, field):
        ca, strip, side, ga, halo_rows, halo_cols = jobs[t]
        high, low = halves(field)
        pooled = mm(high, pool) + mm(low, pool)
        for r in range(packed):
            total = None
            for g in range(groups):
                start = (r * groups + g) * BLOCK
                term = jnp.where(lane_group == g, pooled[start : start + BLOCK], 0.0)
                total = term if total is None else total + term
            ca[r : r + 1] = jnp.sum(total, axis=0, keepdims=True)
        for device in peers:
            remote(ca, ga.at[mine], t, 0, device)
        pltpu.make_async_copy(ca, ga.at[mine], recv_sems.at[t, 0]).start()
        strip[0] = field[:H]
        strip[1] = field[row_count - H :]
        turned = field.T
        side[0] = turned[:H]
        side[1] = turned[col_count - H :]
        for slot, c in ((1, ic), (2, left), (0, right)):
            for tb, a in ((0, up), (1, down)):
                device = {"along": a, "across": c}
                remote(strip.at[tb], halo_rows.at[slot, 1 - tb], t, 1, device)
        remote(side.at[0], halo_cols.at[1], t, 2, {"along": ia, "across": left})
        remote(side.at[1], halo_cols.at[0], t, 2, {"along": ia, "across": right})
        fld[t] = field

    def inside(t):
        centre = (cols_h[col_count : 2 * col_count], cols_l[col_count : 2 * col_count])
        middle = dot3(halves(fld[t]), centre)
        fine[t] = dot3((rows_h[...], rows_l[...]), halves(middle))

    def finish(t):
        ca, strip, side, ga, halo_rows, halo_cols = jobs[t]
        wait_for(halo_rows, recv_sems.at[t, 1])
        wait_for(halo_cols, recv_sems.at[t, 2])
        high, low = halves(jnp.concatenate([halo_cols[0], halo_cols[1]], axis=0).T)
        beside = mm(jnp.concatenate([high, low, high], axis=1), side3[...])
        outer = jnp.concatenate(
            [jnp.concatenate([halo_rows[s, 0], halo_rows[s, 1]], axis=0) for s in range(3)], axis=1
        )
        high, low = halves(dot3(halves(outer), (cols_h[...], cols_l[...])))
        edges = mm(edge3[...], jnp.concatenate([high, low, high], axis=0))
        result = fine[t] + (dot3((rows_h[...], rows_l[...]), halves(beside)) + edges)

        wait_for(ga, recv_sems.at[t, 0])
        theirs = jnp.concatenate(
            [
                jnp.concatenate([ga[a * nc + c] for a in range(na)], axis=0)
                for c in range(nc)
            ],
            axis=1,
        )
        high, low = halves(theirs)
        every = mm(along3[...], jnp.concatenate([high, low, high], axis=0))
        picked = None
        group = iota((coarse_rows, nc * LANES), 1) % LANES // coarse_cols
        for g in range(groups):
            term = jnp.where(group == g, every[g * coarse_rows : (g + 1) * coarse_rows], 0.0)
            picked = term if picked is None else picked + term
        back = dot3(halves(picked), (across_h[...], across_l[...]))
        return result + jnp.concatenate(
            [jnp.broadcast_to(back[p : p + 1], (BLOCK, col_count)) for p in range(coarse_rows)],
            axis=0,
        )

    shots = doses_ref.shape[-1]
    share = kinds / shots
    live = (iota((1, shots), 1) < count_ref[...]).astype(jnp.float32)
    chosen = (type_ref[0] == iota((kinds, shots), 0)).astype(jnp.float32)
    coef0 = share * jnp.broadcast_to(
        jnp.sum(chosen * (live * doses_ref[0]), axis=1, keepdims=True), (kinds, col_count)
    )
    for kind in range(kinds):
        wf[kind] = w_ref[kind].astype(jnp.float32)
    first = dose_map(coef0)

    pl.semaphore_wait(barrier, len(peers))
    send(0, first)
    send(COTANGENT, cot_ref[...])

    shape = (col_count, col_count)
    gap = iota(shape, 1) - iota(shape, 0)
    lefts = jnp.where(ic > 0, fine_weight(gap + col_count), 0.0)
    rights = jnp.where(ic < nc - 1, fine_weight(gap - col_count), 0.0)
    cols_h[...], cols_l[...] = halves(jnp.concatenate([lefts, fine_weight(gap), rights], axis=0))
    high, low = halves(jnp.concatenate([lefts[col_count - H :], rights[:H]], axis=0))
    side3[...] = jnp.concatenate([high, high, low], axis=0)
    shape = (row_count, row_count)
    rows_h[...], rows_l[...] = halves(fine_weight(iota(shape, 0) - iota(shape, 1)))
    shape = (row_count, 2 * H)
    spot = iota(shape, 1)
    above = jnp.where(ia > 0, fine_weight(iota(shape, 0) - (spot - H)), 0.0)
    below = jnp.where(ia < na - 1, fine_weight(iota(shape, 0) - (spot - H + row_count)), 0.0)
    high, low = halves(jnp.where(spot < H, above, below))
    edge3[...] = jnp.concatenate([high, high, low], axis=1)
    shape = (groups * coarse_rows, na * packed)
    target = ia * coarse_rows + iota(shape, 0) % coarse_rows
    high, low = halves(back_weight(target - (iota(shape, 1) * groups + iota(shape, 0) // coarse_rows)))
    along3[...] = jnp.concatenate([high, high, low], axis=1)
    shape = (nc * LANES, col_count)
    source = iota(shape, 0) // LANES * coarse_cols + iota(shape, 0) % coarse_cols
    across_h[...], across_l[...] = halves(
        back_weight(source - (ic * coarse_cols + iota(shape, 1) // BLOCK), back_ratio)
    )
    totals = weighted(None)

    inside(0)
    ratio0 = weighted(finish(0)) / totals
    coef1 = coef0 / ratio0
    send(1, dose_map(coef1))

    inside(1)
    inside(COTANGENT)
    grad2 = weighted(finish(COTANGENT))
    ratio1 = weighted(finish(1)) / totals
    coef2 = coef1 / ratio1
    grad_ratio1 = -grad2 * coef2 / ratio1
    send(2, dose_map(grad_ratio1 / totals))
    send(EXPOSURE, dose_map(coef2))

    inside(2)
    grad1 = grad2 / ratio1 + weighted(finish(2))
    grad_ratio0 = -grad1 * coef1 / ratio0
    send(3, dose_map(grad_ratio0 / totals))

    inside(3)
    inside(EXPOSURE)
    out_ref[...] = finish(EXPOSURE)
    grad0 = grad1 / ratio0 + weighted(finish(3))
    grad_ref[0] = live * share * jnp.sum(chosen * grad0[:, 0:1], axis=0, keepdims=True)

    for t in range(JOBS):
        ca, strip, side, ga, halo_rows, halo_cols = jobs[t]
        wait_for(ga.at[: na * nc - 1], send_sems.at[t, 0])
        wait_for(halo_rows, send_sems.at[t, 1])
        wait_for(halo_cols, send_sems.at[t, 2])


def shards(na, nc, doses, shot_type, shot_count, dose_weights, cotangent):
    kinds, rows, cols = dose_weights.shape
    f32, bf16 = jnp.float32, jnp.bfloat16
    coarse_rows = rows // BLOCK
    packed = coarse_rows * (cols // BLOCK) // LANES

    def pair(*shape):
        return [pltpu.VMEM(shape, bf16), pltpu.VMEM(shape, bf16)]

    scratch = [pltpu.VMEM((kinds, rows, cols), f32)] + [pltpu.VMEM((JOBS, rows, cols), f32)] * 2
    scratch += pair(3 * cols, cols) + [pltpu.VMEM((6 * H, cols), bf16)]
    scratch += pair(rows, rows) + [pltpu.VMEM((rows, 6 * H), bf16)]
    groups = coarse_rows // packed
    scratch += [pltpu.VMEM((groups * coarse_rows, 3 * na * packed), bf16)] + pair(nc * LANES, cols)
    for _ in range(JOBS):
        scratch += [
            pltpu.VMEM((packed, LANES), f32),
            pltpu.VMEM((2, H, cols), f32),
            pltpu.VMEM((2, H, rows), f32),
            pltpu.VMEM((na * nc, packed, LANES), f32),
            pltpu.VMEM((3, 2, H, cols), f32),
            pltpu.VMEM((2, H, rows), f32),
        ]
    scratch += [pltpu.SemaphoreType.DMA((JOBS, 3)), pltpu.SemaphoreType.DMA((JOBS, 3))]
    return pl.pallas_call(
        functools.partial(kernel, na, nc),
        out_shape=(
            jax.ShapeDtypeStruct(cotangent.shape, f32),
            jax.ShapeDtypeStruct(doses.shape, f32),
        ),
        in_specs=[pl.BlockSpec(memory_space=pltpu.VMEM)] * 5,
        out_specs=(pl.BlockSpec(memory_space=pltpu.VMEM),) * 2,
        scratch_shapes=scratch,
        compiler_params=pltpu.CompilerParams(
            collective_id=0, has_side_effects=True, vmem_limit_bytes=32 * 1024 * 1024
        ),
    )(doses, shot_type, shot_count, dose_weights, cotangent)


def solution(mesh):
    in_specs = (
        P(("groups", "along"), "across", None),
        P(("groups", "along"), "across", None),
        P(("groups", "along"), "across"),
        P(None, ("groups", "along"), "across"),
        P(("groups", "along"), "across"),
    )
    out_specs = (P(("groups", "along"), "across"), P(("groups", "along"), "across", None))
    run = functools.partial(shards, mesh.shape["along"], mesh.shape["across"])
    return jax.shard_map(run, mesh=mesh, in_specs=in_specs, out_specs=out_specs, check_vma=False)
```

time: 43.8 us -> 40.3 us (0.920)
  Pallas kernels: 37.8 us -> 34.2 us
    pallas_call x1, Pallas kernels: 37.8 us -> 34.2 us  [shards(): pl.pallas_call(functools.partial(kernel, na, nc), out_shape=(jax.ShapeDty...]
where the time goes in v2:
time: 40.3 us; the launch traced here: 40.1 us
  Pallas kernels  34.2 us (85%)
  local copies, waits for them, and re-layouts  4.54 us (11%)
  between operations  1.3 us (3%)
    pallas_call x1, Pallas kernels, shards(): pl.pallas_call(functools.partial(kernel, na, nc), out_shape=(jax.ShapeDty...  34.2 us
    unnamed x10, local copies, waits for them, and re-layouts  4.54 us

profile of v2, /device:TPU:0, one launch (start us, length us, event | category | flops | bytes accessed | tf_op | source)
XLA Modules:
  0.0 40.1 jit_solution(12668175953532024975)
XLA Ops:
  1.3 0.0 copy-start
  1.3 1.0 %copy-done = bf16[8,256,128]{2,1,0:T(8,128)(2,1)S(1)} copy-done((bf16[8,256,128]{2,1,0:T(8,128)(2,1)S(1)}, bf16[8,256,128]{2,1,0:T(8,128)(2,1)}, u32[]{:S(2)}) %copy-start) | copy-done | bytes 524312
  2.3 0.0 copy-start.1
  2.3 0.9 %copy-done.1 = f32[256,128]{1,0:T(8,128)S(1)} copy-done((f32[256,128]{1,0:T(8,128)S(1)}, f32[256,128]{1,0:T(8,128)}, u32[]{:S(2)}) %copy-start.1) | copy-done | bytes 131096
  3.2 0.0 copy-start.2
  3.2 0.7 %copy-done.2 = f32[1,1,512]{2,1,0:T(1,128)S(1)} copy-done((f32[1,1,512]{2,1,0:T(1,128)S(1)}, f32[1,1,512]{2,1,0:T(1,128)}, u32[]{:S(2)}) %copy-start.2) | copy-done | bytes 2072
  3.9 0.0 copy-start.3
  3.9 0.7 %copy-done.3 = s32[1,1,512]{2,1,0:T(1,128)S(1)} copy-done((s32[1,1,512]{2,1,0:T(1,128)S(1)}, s32[1,1,512]{2,1,0:T(1,128)}, u32[]{:S(2)}) %copy-start.3) | copy-done | bytes 2072
  4.6 34.2 %shard_map.68 = (f32[256,128]{1,0:T(8,128)S(1)}, f32[1,1,512]{2,1,0:T(1,128)S(1)}) custom-call(f32[1,1,512]{2,1,0:T(1,128)S(1)} %copy-done.2, s32[1,1,512]{2,1,0:T(1,128)S(1)} %copy-done.3, s32[1,1]{1,0:T(1,128)S(6)} %copy.9.refs_2_, bf16[8,256,128]{2,1,0:T(8,128)(2,1)S(1)} %copy-done, f32[256,128]{1,0:T(8,128)S(1)} %copy-done.1), custom_call_target="tpu_custom_call" | custom-call | tf_op jit(solution)/shard_map/pallas_call | solution.py:286
  38.8 0.7 %copy.10 = f32[256,128]{1,0:T(8,128)} copy(f32[256,128]{1,0:T(8,128)S(1)} %get-tuple-element.4) | data formatting | bytes 262144
  39.5 0.6 %copy.11 = f32[1,1,512]{2,1,0:T(1,128)} copy(f32[1,1,512]{2,1,0:T(1,128)S(1)} %get-tuple-element.5) | data formatting | bytes 4096
Async XLA Ops:
  1.3 1.0 %copy-start = (bf16[8,256,128]{2,1,0:T(8,128)(2,1)S(1)}, bf16[8,256,128]{2,1,0:T(8,128)(2,1)}, u32[]{:S(2)}) copy-start(bf16[8,256,128]{2,1,0:T(8,128)(2,1)} %refs_3_.1) | copy-start | bytes 1572868
  2.3 0.9 %copy-start.1 = (f32[256,128]{1,0:T(8,128)S(1)}, f32[256,128]{1,0:T(8,128)}, u32[]{:S(2)}) copy-start(f32[256,128]{1,0:T(8,128)} %refs_4_.1) | copy-start | bytes 393220
  3.2 0.7 %copy-start.2 = (f32[1,1,512]{2,1,0:T(1,128)S(1)}, f32[1,1,512]{2,1,0:T(1,128)}, u32[]{:S(2)}) copy-start(f32[1,1,512]{2,1,0:T(1,128)} %refs_0_.1) | copy-start | bytes 6148
  3.9 0.7 %copy-start.3 = (s32[1,1,512]{2,1,0:T(1,128)S(1)}, s32[1,1,512]{2,1,0:T(1,128)}, u32[]{:S(2)}) copy-start(s32[1,1,512]{2,1,0:T(1,128)} %refs_1_.1) | copy-start | bytes 6148

commit v3 on v2

--- a/solution.py
+++ b/solution.py
@@ -53,12 +53,19 @@
 
 
 def kernel(na, nc, *refs):
-    doses_ref, type_ref, count_ref, w_ref, cot_ref, out_ref, grad_ref = refs[:7]
+    *sources, out_ref, grad_ref = refs[:7]
     (
         wf, fld, fine, cols_h, cols_l, side3, rows_h, rows_l, edge3, along3, across_h, across_l,
     ) = refs[7:19]
     jobs = [refs[19 + 6 * t : 25 + 6 * t] for t in range(JOBS)]
-    send_sems, recv_sems = refs[19 + 6 * JOBS :]
+    send_sems, recv_sems, load_sems, *held = refs[19 + 6 * JOBS :]
+    doses_ref, type_ref, count_ref, w_ref, cot_ref = held
+    loads = [
+        pltpu.make_async_copy(source, target, load_sems.at[n])
+        for n, (source, target) in enumerate(zip(sources, held))
+    ]
+    for n in (3, 0, 1, 2, 4):
+        loads[n].start()
     kinds, row_count, col_count = w_ref.shape
     coarse_rows = row_count // BLOCK
     coarse_cols = col_count // BLOCK
@@ -186,21 +193,6 @@
             axis=0,
         )
 
-    shots = doses_ref.shape[-1]
-    share = kinds / shots
-    live = (iota((1, shots), 1) < count_ref[...]).astype(jnp.float32)
-    chosen = (type_ref[0] == iota((kinds, shots), 0)).astype(jnp.float32)
-    coef0 = share * jnp.broadcast_to(
-        jnp.sum(chosen * (live * doses_ref[0]), axis=1, keepdims=True), (kinds, col_count)
-    )
-    for kind in range(kinds):
-        wf[kind] = w_ref[kind].astype(jnp.float32)
-    first = dose_map(coef0)
-
-    pl.semaphore_wait(barrier, len(peers))
-    send(0, first)
-    send(COTANGENT, cot_ref[...])
-
     shape = (col_count, col_count)
     gap = iota(shape, 1) - iota(shape, 0)
     lefts = jnp.where(ic > 0, fine_weight(gap + col_count), 0.0)
@@ -210,6 +202,24 @@
     side3[...] = jnp.concatenate([high, high, low], axis=0)
     shape = (row_count, row_count)
     rows_h[...], rows_l[...] = halves(fine_weight(iota(shape, 0) - iota(shape, 1)))
+    for load in loads[:4]:
+        load.wait()
+    shots = doses_ref.shape[-1]
+    share = kinds / shots
+    live = (iota((1, shots), 1) < count_ref[...]).astype(jnp.float32)
+    chosen = (type_ref[0] == iota((kinds, shots), 0)).astype(jnp.float32)
+    coef0 = share * jnp.broadcast_to(
+        jnp.sum(chosen * (live * doses_ref[0]), axis=1, keepdims=True), (kinds, col_count)
+    )
+    for kind in range(kinds):
+        wf[kind] = w_ref[kind].astype(jnp.float32)
+    first = dose_map(coef0)
+
+    pl.semaphore_wait(barrier, len(peers))
+    send(0, first)
+    loads[4].wait()
+    send(COTANGENT, cot_ref[...])
+
     shape = (row_count, 2 * H)
     spot = iota(shape, 1)
     above = jnp.where(ia > 0, fine_weight(iota(shape, 0) - (spot - H)), 0.0)
@@ -283,19 +293,22 @@
             pltpu.VMEM((2, H, rows), f32),
         ]
     scratch += [pltpu.SemaphoreType.DMA((JOBS, 3)), pltpu.SemaphoreType.DMA((JOBS, 3))]
+    operands = (doses, shot_type, shot_count, dose_weights, cotangent)
+    scratch += [pltpu.SemaphoreType.DMA((len(operands),))]
+    scratch += [pltpu.VMEM(operand.shape, operand.dtype) for operand in operands]
     return pl.pallas_call(
         functools.partial(kernel, na, nc),
         out_shape=(
             jax.ShapeDtypeStruct(cotangent.shape, f32),
             jax.ShapeDtypeStruct(doses.shape, f32),
         ),
-        in_specs=[pl.BlockSpec(memory_space=pltpu.VMEM)] * 5,
+        in_specs=[pl.BlockSpec(memory_space=pltpu.HBM)] * 5,
         out_specs=(pl.BlockSpec(memory_space=pltpu.VMEM),) * 2,
         scratch_shapes=scratch,
         compiler_params=pltpu.CompilerParams(
-            collective_id=0, has_side_effects=True, vmem_limit_bytes=32 * 1024 * 1024
+            collective_id=0, has_side_effects=True, vmem_limit_bytes=64 * 1024 * 1024
         ),
-    )(doses, shot_type, shot_count, dose_weights, cotangent)
+    )(*operands)
 
 
 def solution(mesh):

time: 40.3 us -> 38.6 us (0.958)
  local copies, waits for them, and re-layouts: 4.54 us -> 2.15 us
  Pallas kernels: 34.2 us -> 35 us
    unnamed x10 -> x4, local copies, waits for them, and re-layouts: 4.54 us -> 2.15 us
    pallas_call x1, Pallas kernels: 34.2 us -> 35 us  [shards(): pl.pallas_call(functools.partial(kernel, na, nc), out_shape=(jax.ShapeDty...]
where the time goes in v3:
time: 38.6 us; the launch traced here: 38.4 us
  Pallas kernels  35 us (91%)
  local copies, waits for them, and re-layouts  2.15 us (6%)
  between operations  1.29 us (3%)
    pallas_call x1, Pallas kernels, shards(): pl.pallas_call(functools.partial(kernel, na, nc), out_shape=(jax.ShapeDty...  35 us
    unnamed x4, local copies, waits for them, and re-layouts  2.15 us

profile of v3, /device:TPU:0, one launch (start us, length us, event | category | flops | bytes accessed | tf_op | source)
XLA Modules:
  0.0 38.4 jit_solution(18401437539129803981)
XLA Ops:
  1.3 35.0 %shard_map.68 = (f32[256,128]{1,0:T(8,128)}, f32[1,1,512]{2,1,0:T(1,128)}) custom-call(f32[1,1,512]{2,1,0:T(1,128)} %refs_0_.1, s32[1,1,512]{2,1,0:T(1,128)} %refs_1_.1, s32[1,1]{1,0:T(1,128)S(6)} %copy.9.refs_2_, bf16[8,256,128]{2,1,0:T(8,128)(2,1)} %refs_3_.1, f32[256,128]{1,0:T(8,128)} %refs_4_.1), custom_call_target="tpu_custom_call" | custom-call | tf_op jit(solution)/shard_map/pallas_call | solution.py:299
  36.3 0.0 copy-start
  36.3 1.6 %copy.10 = f32[256,128]{1,0:T(8,128)} copy(f32[256,128]{1,0:T(8,128)} %get-tuple-element.4) | data formatting | bytes 262144
  37.9 0.0 copy-done
  37.9 0.6 %copy.11 = f32[1,1,512]{2,1,0:T(1,128)} copy(f32[1,1,512]{2,1,0:T(1,128)S(1)} %copy-done) | data formatting | bytes 4096
Async XLA Ops:
  36.3 1.6 %copy-start = (f32[1,1,512]{2,1,0:T(1,128)S(1)}, f32[1,1,512]{2,1,0:T(1,128)}, u32[]{:S(2)}) copy-start(f32[1,1,512]{2,1,0:T(1,128)} %get-tuple-element.5) | copy-start | bytes 6148

commit v4 on v3

--- a/solution.py
+++ b/solution.py
@@ -85,6 +85,15 @@
         if oa or oc
     ]
 
+    has_up, has_down = ia > 0, ia < na - 1
+
+    for tb, edge in ((0, ia == 0), (1, ia == na - 1)):
+
+        @pl.when(edge)
+        def _():
+            for t in range(JOBS):
+                jobs[t][4][tb] = jnp.zeros(jobs[t][4].shape[1:], jnp.float32)
+
     barrier = pltpu.get_barrier_semaphore()
     for device in peers:
         pl.semaphore_signal(barrier, inc=1, device_id=device, device_id_type=pl.DeviceIdType.MESH)
@@ -146,12 +155,16 @@
         turned = field.T
         side[0] = turned[:H]
         side[1] = turned[col_count - H :]
-        for slot, c in ((1, ic), (2, left), (0, right)):
-            for tb, a in ((0, up), (1, down)):
-                device = {"along": a, "across": c}
-                remote(strip.at[tb], halo_rows.at[slot, 1 - tb], t, 1, device)
-        remote(side.at[0], halo_cols.at[1], t, 2, {"along": ia, "across": left})
-        remote(side.at[1], halo_cols.at[0], t, 2, {"along": ia, "across": right})
+        for tb, a, some in ((0, up, has_up), (1, down, has_down)):
+
+            @pl.when(some)
+            def _():
+                for slot, c in ((1, ic), (2, left), (0, right)):
+                    device = {"along": a, "across": c}
+                    remote(strip.at[tb], halo_rows.at[1 - tb, slot], t, 2 - tb, device)
+
+        remote(side.at[0], halo_cols.at[1], t, 3, {"along": ia, "across": left})
+        remote(side.at[1], halo_cols.at[0], t, 3, {"along": ia, "across": right})
         fld[t] = field
 
     def inside(t):
@@ -161,12 +174,17 @@
 
     def finish(t):
         ca, strip, side, ga, halo_rows, halo_cols = jobs[t]
-        wait_for(halo_rows, recv_sems.at[t, 1])
-        wait_for(halo_cols, recv_sems.at[t, 2])
+        for tb, some in ((0, has_up), (1, has_down)):
+
+            @pl.when(some)
+            def _():
+                wait_for(halo_rows.at[tb], recv_sems.at[t, 1 + tb])
+
+        wait_for(halo_cols, recv_sems.at[t, 3])
         high, low = halves(jnp.concatenate([halo_cols[0], halo_cols[1]], axis=0).T)
         beside = mm(jnp.concatenate([high, low, high], axis=1), side3[...])
         outer = jnp.concatenate(
-            [jnp.concatenate([halo_rows[s, 0], halo_rows[s, 1]], axis=0) for s in range(3)], axis=1
+            [jnp.concatenate([halo_rows[0, s], halo_rows[1, s]], axis=0) for s in range(3)], axis=1
         )
         high, low = halves(dot3(halves(outer), (cols_h[...], cols_l[...])))
         edges = mm(edge3[...], jnp.concatenate([high, low, high], axis=0))
@@ -265,8 +283,13 @@
     for t in range(JOBS):
         ca, strip, side, ga, halo_rows, halo_cols = jobs[t]
         wait_for(ga.at[: na * nc - 1], send_sems.at[t, 0])
-        wait_for(halo_rows, send_sems.at[t, 1])
-        wait_for(halo_cols, send_sems.at[t, 2])
+        for tb, some in ((0, has_down), (1, has_up)):
+
+            @pl.when(some)
+            def _():
+                wait_for(halo_rows.at[tb], send_sems.at[t, 1 + tb])
+
+        wait_for(halo_cols, send_sems.at[t, 3])
 
 
 def shards(na, nc, doses, shot_type, shot_count, dose_weights, cotangent):
@@ -289,10 +312,10 @@
             pltpu.VMEM((2, H, cols), f32),
             pltpu.VMEM((2, H, rows), f32),
             pltpu.VMEM((na * nc, packed, LANES), f32),
-            pltpu.VMEM((3, 2, H, cols), f32),
+            pltpu.VMEM((2, 3, H, cols), f32),
             pltpu.VMEM((2, H, rows), f32),
         ]
-    scratch += [pltpu.SemaphoreType.DMA((JOBS, 3)), pltpu.SemaphoreType.DMA((JOBS, 3))]
+    scratch += [pltpu.SemaphoreType.DMA((JOBS, 4)), pltpu.SemaphoreType.DMA((JOBS, 4))]
     operands = (doses, shot_type, shot_count, dose_weights, cotangent)
     scratch += [pltpu.SemaphoreType.DMA((len(operands),))]
     scratch += [pltpu.VMEM(operand.shape, operand.dtype) for operand in operands]

time: 38.6 us -> 35.5 us (0.920)
  Pallas kernels: 35 us -> 31.9 us
    pallas_call x1, Pallas kernels: 35 us -> 31.9 us  [shards(): pl.pallas_call(functools.partial(kernel, na, nc), out_shape=(jax.ShapeDty...]
where the time goes in v4:
time: 35.5 us; the launch traced here: 35.4 us
  Pallas kernels  31.9 us (90%)
  local copies, waits for them, and re-layouts  2.15 us (6%)
  between operations  1.29 us (4%)
    pallas_call x1, Pallas kernels, shards(): pl.pallas_call(functools.partial(kernel, na, nc), out_shape=(jax.ShapeDty...  31.9 us
    unnamed x4, local copies, waits for them, and re-layouts  2.15 us

profile of v4, /device:TPU:0, one launch (start us, length us, event | category | flops | bytes accessed | tf_op | source)
XLA Modules:
  0.0 35.4 jit_solution(5242222792621162479)
XLA Ops:
  1.3 31.9 %shard_map.68 = (f32[256,128]{1,0:T(8,128)}, f32[1,1,512]{2,1,0:T(1,128)}) custom-call(f32[1,1,512]{2,1,0:T(1,128)} %refs_0_.1, s32[1,1,512]{2,1,0:T(1,128)} %refs_1_.1, s32[1,1]{1,0:T(1,128)S(6)} %copy.9.refs_2_, bf16[8,256,128]{2,1,0:T(8,128)(2,1)} %refs_3_.1, f32[256,128]{1,0:T(8,128)} %refs_4_.1), custom_call_target="tpu_custom_call" | custom-call | tf_op jit(solution)/shard_map/pallas_call | solution.py:322
  33.2 0.0 copy-start
  33.2 1.6 %copy.10 = f32[256,128]{1,0:T(8,128)} copy(f32[256,128]{1,0:T(8,128)} %get-tuple-element.4) | data formatting | bytes 262144
  34.8 0.0 copy-done
  34.8 0.6 %copy.11 = f32[1,1,512]{2,1,0:T(1,128)} copy(f32[1,1,512]{2,1,0:T(1,128)S(1)} %copy-done) | data formatting | bytes 4096
Async XLA Ops:
  33.2 1.6 %copy-start = (f32[1,1,512]{2,1,0:T(1,128)S(1)}, f32[1,1,512]{2,1,0:T(1,128)}, u32[]{:S(2)}) copy-start(f32[1,1,512]{2,1,0:T(1,128)} %get-tuple-element.5) | copy-start | bytes 6148

commit v5 on v4

--- a/solution.py
+++ b/solution.py
@@ -236,7 +236,6 @@
     pl.semaphore_wait(barrier, len(peers))
     send(0, first)
     loads[4].wait()
-    send(COTANGENT, cot_ref[...])
 
     shape = (row_count, 2 * H)
     spot = iota(shape, 1)
@@ -256,6 +255,7 @@
     totals = weighted(None)
 
     inside(0)
+    send(COTANGENT, cot_ref[...])
     ratio0 = weighted(finish(0)) / totals
     coef1 = coef0 / ratio0
     send(1, dose_map(coef1))
@@ -267,9 +267,9 @@
     coef2 = coef1 / ratio1
     grad_ratio1 = -grad2 * coef2 / ratio1
     send(2, dose_map(grad_ratio1 / totals))
+
+    inside(2)
     send(EXPOSURE, dose_map(coef2))
-
-    inside(2)
     grad1 = grad2 / ratio1 + weighted(finish(2))
     grad_ratio0 = -grad1 * coef1 / ratio0
     send(3, dose_map(grad_ratio0 / totals))

time: 35.5 us -> 35.5 us (level)
  no operation moved by 1% of the time
where the time goes in v5:
time: 35.5 us; the launch traced here: 35.4 us
  Pallas kernels  31.9 us (90%)
  local copies, waits for them, and re-layouts  2.15 us (6%)
  between operations  1.29 us (4%)
    pallas_call x1, Pallas kernels, shards(): pl.pallas_call(functools.partial(kernel, na, nc), out_shape=(jax.ShapeDty...  31.9 us
    unnamed x4, local copies, waits for them, and re-layouts  2.15 us

profile of v5, /device:TPU:0, one launch (start us, length us, event | category | flops | bytes accessed | tf_op | source)
XLA Modules:
  0.0 35.4 jit_solution(6699892599623664119)
XLA Ops:
  1.3 31.9 %shard_map.68 = (f32[256,128]{1,0:T(8,128)}, f32[1,1,512]{2,1,0:T(1,128)}) custom-call(f32[1,1,512]{2,1,0:T(1,128)} %refs_0_.1, s32[1,1,512]{2,1,0:T(1,128)} %refs_1_.1, s32[1,1]{1,0:T(1,128)S(6)} %copy.9.refs_2_, bf16[8,256,128]{2,1,0:T(8,128)(2,1)} %refs_3_.1, f32[256,128]{1,0:T(8,128)} %refs_4_.1), custom_call_target="tpu_custom_call" | custom-call | tf_op jit(solution)/shard_map/pallas_call | solution.py:322
  33.2 0.0 copy-start
  33.2 1.6 %copy.10 = f32[256,128]{1,0:T(8,128)} copy(f32[256,128]{1,0:T(8,128)} %get-tuple-element.4) | data formatting | bytes 262144
  34.8 0.0 copy-done
  34.8 0.6 %copy.11 = f32[1,1,512]{2,1,0:T(1,128)} copy(f32[1,1,512]{2,1,0:T(1,128)S(1)} %copy-done) | data formatting | bytes 4096
Async XLA Ops:
  33.2 1.6 %copy-start = (f32[1,1,512]{2,1,0:T(1,128)S(1)}, f32[1,1,512]{2,1,0:T(1,128)}, u32[]{:S(2)}) copy-start(f32[1,1,512]{2,1,0:T(1,128)} %get-tuple-element.5) | copy-start | bytes 6148
